TPU v7x, 256 devices: a whole 4x4x8 slice. The times are simulated.
256 devices in a mesh: ctx: 32 (over z, x), ep: 8 (over y, core).
Axes of the slice: x: 4, y: 4, z: 8, core: 2. Of those that a mesh axis runs over, the one named last changes fastest.
Arguments:
- lin_query: bfloat16 [8192, 4096], P('ctx', 'ep'), may hold values from -6 to 6
- lin_keys: bfloat16 [8192, 4096], P('ctx', 'ep'), may hold values from -0.5 to 0.5
- lin_values: bfloat16 [8192, 4096], P('ctx', 'ep'), may hold values from -6 to 6
- log_decay: float32 [8192, 32], P('ctx', 'ep'), may hold values from -1 to 0
- soft_query: bfloat16 [8192, 4096], P('ctx', 'ep'), may hold values from -80 to 80
- soft_keys: bfloat16 [8192, 1024], P('ctx', 'ep'), may hold values from -4 to 4
- soft_values: bfloat16 [8192, 1024], P('ctx', 'ep'), may hold values from -6 to 6
- key_lists: int32 [64, 8], P('ctx'), may hold values from 0 to 63, as said below
- moe_input: bfloat16 [512, 6144], P('ctx'), may hold values from -6 to 6
- expert_ids: int32 [512, 2], P('ctx'), may hold values from 0 to 7, all different within a row; in each aligned block of 16 rows (0 to 15, 16 to 31, ...) at most 8 rows name the same one
- expert_gates: bfloat16 [512, 2], P('ctx'), may hold values from 0.19921875 to 1
- gate_proj: bfloat16 [8, 6144, 9216], P('ep', None, 'ctx'), may hold values from -0.078125 to 0.078125
- up_proj: bfloat16 [8, 6144, 9216], P('ep', None, 'ctx'), may hold values from -0.078125 to 0.078125
- down_proj: bfloat16 [8, 9216, 6144], P('ep', 'ctx'), may hold values from -0.0625 to 0.0625
Outputs:
- lin_mixed: bfloat16 [8192, 4096], P('ctx', 'ep')
- soft_mixed: bfloat16 [8192, 4096], P('ctx', 'ep')
- expert_mixed: bfloat16 [512, 6144], P('ctx')
Inputs may be any that keep to these rules, and one draw needn't show every extreme that they name: `key_lists`: the 8 key-block numbers of a query block are distinct and include the query block's own number. `expert_ids`: A token's 2 experts are distinct. Among the 16 tokens of one index of ctx no expert is named by more than 8 tokens, and in every draw some expert is named by exactly 8 of them.
All inputs are finite; a program needn't handle non-finite values.
Results may differ from a plain program's by a relative error of at most 0.023.
Values may be sent and summed in bfloat16 or wider, within the bound.
No kernel may reach another device: no remote copies, remote signals or barrier semaphores. Data moves between devices by JAX's collectives and lax.ppermute only.
A program may use at most 128 MiB of HBM per device.

v0:
```python
import math

import jax
import jax.numpy as jnp
from jax import lax
from jax.sharding import PartitionSpec as P

HD = 128
BLK = 128
CAP = 8


def carried_in_2(x, axis, join, neutral):
    place = lax.axis_index(axis)
    gathered = jax.tree.map(
        lambda a, kind: lax.all_gather(a.astype(kind), axis), x, (jnp.bfloat16, jnp.bfloat16)
    )
    state = jax.tree.map(lambda a, e: jnp.zeros_like(a) + jnp.asarray(e, a.dtype), x, neutral)

    def one(turn, state):
        return join(
            state,
            jax.tree.map(
                lambda a, own: lax.dynamic_index_in_dim(a, turn, 0, False).astype(own.dtype),
                gathered,
                x,
            ),
        )

    return lax.fori_loop(0, place, one, state)


def lightning_part(lin_query, lin_keys, lin_values, log_decay):
    heads = log_decay.shape[1]
    tok_rows = lin_query.shape[0]
    query_plain = lin_query.reshape(tok_rows, heads, HD)
    key_plain = lin_keys.reshape(tok_rows, heads, HD)
    value_plain = lin_values.reshape(tok_rows, heads, HD)
    query_rows = query_plain.astype(jnp.float32)
    cumul = jnp.cumsum(log_decay, axis=0)
    positions = jnp.arange(tok_rows, dtype=jnp.int32)
    causal = (positions[:, None] >= positions[None, :])[:, :, None]
    spread = cumul[:, None, :] - cumul[None, :, :]
    weight = jnp.where(causal, jnp.exp(jnp.where(causal, spread, 0.0)), 0.0)
    scores = (
        jnp.einsum("thd,shd->tsh", query_plain, key_plain, preferred_element_type=jnp.float32)
        * weight
    )
    inside = jnp.einsum(
        "tsh,she->the", scores.astype(jnp.bfloat16), value_plain, preferred_element_type=jnp.float32
    )
    ending = cumul[-1]
    carried = (jnp.exp(ending[None, :] - cumul)[:, :, None] * key_plain.astype(jnp.float32)).astype(
        jnp.bfloat16
    )
    local_state = jnp.einsum(
        "shd,she->hde", carried, value_plain, preferred_element_type=jnp.float32
    )
    local_decay = jnp.exp(ending)

    def chain(earlier, later):
        return (earlier[0] * later[0], later[0][:, None, None] * earlier[1] + later[1])

    neutral = (jnp.ones_like(local_decay), jnp.zeros_like(local_state))
    _, incoming = carried_in_2((local_decay, local_state), "ctx", chain, neutral)
    carried_in = jnp.exp(cumul)[:, :, None] * jnp.einsum(
        "thd,hde->the", query_rows, incoming, precision=lax.Precision.HIGHEST
    )
    output_rows = inside + carried_in
    output_rows = output_rows * lax.rsqrt(
        jnp.mean(output_rows * output_rows, axis=-1, keepdims=True) + 1e-05
    )
    return output_rows.reshape(tok_rows, heads * HD).astype(jnp.bfloat16)


def softmax_part(soft_query, soft_keys, soft_values, key_lists):
    kv_heads = soft_keys.shape[1] // HD
    query_heads = soft_query.shape[1] // HD
    groups = query_heads // kv_heads
    tok_rows = soft_query.shape[0]
    scaling = float(HD) ** (-0.5)
    query_grid = soft_query.reshape(tok_rows, kv_heads, groups, HD)
    start_state = (
        jnp.full((kv_heads, groups, tok_rows), -1e30, jnp.float32),
        jnp.zeros((kv_heads, groups, tok_rows), jnp.float32),
        jnp.zeros((kv_heads, groups, tok_rows, HD), jnp.float32),
    )
    carry_state = start_state
    key_piece = lax.all_gather(soft_keys, "ctx", axis=0, tiled=True)
    value_piece = lax.all_gather(soft_values, "ctx", axis=0, tiled=True)
    row_count = key_piece.shape[0]
    width = math.gcd(row_count, 512)
    windows = row_count // width
    key_parts = key_piece.reshape(windows, width, kv_heads, HD)
    value_parts = value_piece.reshape(windows, width, kv_heads, HD)
    offsets = jnp.arange(windows, dtype=jnp.int32) * width

    def visit(carry, item):
        key_block, value_block, offset = item
        best, denom, accum = carry
        key_ids = (offset + jnp.arange(width, dtype=jnp.int32)) // BLK
        allowed = jnp.any(key_lists[:, :, None] == key_ids[None, None, :], axis=1)
        allowed = jnp.repeat(allowed, BLK, axis=0)[None, None]
        scores = (
            jnp.einsum("tkgd,skd->kgts", query_grid, key_block, preferred_element_type=jnp.float32)
            * scaling
        )
        scores = jnp.where(allowed, scores, -1e30)
        newest = jnp.maximum(best, jnp.max(scores, axis=-1))
        weights = jnp.where(allowed, jnp.exp(scores - newest[..., None]), 0.0)
        shrink = jnp.exp(best - newest)
        denom = denom * shrink + jnp.sum(weights, axis=-1)
        accum = accum * shrink[..., None] + jnp.einsum(
            "kgts,skd->kgtd",
            weights.astype(jnp.bfloat16),
            value_block,
            preferred_element_type=jnp.float32,
        )
        return ((newest, denom, accum), None)

    carry_state, _ = lax.scan(visit, carry_state, (key_parts, value_parts, offsets))
    best, denom, accum = carry_state
    mixed = jnp.transpose(accum / denom[..., None], (2, 0, 1, 3))
    return mixed.reshape(tok_rows, query_heads * HD).astype(jnp.bfloat16)


def slot_table(id_rows, gate_rows, experts_here):
    match = id_rows[:, None, :] == experts_here[None, :, None]
    routed = jnp.any(match, axis=2).astype(jnp.int32)
    token_gate = jnp.sum(jnp.where(match, gate_rows.astype(jnp.float32)[:, None, :], 0.0), axis=2)
    places = jnp.cumsum(routed, axis=0) - 1
    onehot = (
        jnp.transpose(places)[:, None, :] == jnp.arange(CAP, dtype=jnp.int32)[None, :, None]
    ) & (jnp.transpose(routed)[:, None, :] > 0)
    return (onehot, token_gate)


def pick_rows(onehot, token_rows):
    return jnp.einsum(
        "ecm,md->ced", onehot.astype(jnp.bfloat16), token_rows, preferred_element_type=jnp.float32
    ).astype(jnp.bfloat16)


def expert_part(moe_input, expert_ids, expert_gates, gate_proj, up_proj, down_proj):
    local_experts = gate_proj.shape[0]
    experts_here = lax.axis_index("ep") * local_experts + jnp.arange(local_experts, dtype=jnp.int32)
    onehot, token_gate = slot_table(expert_ids, expert_gates, experts_here)
    all_tokens, all_gates = (
        lax.all_gather(moe_input, "ctx", axis=0, tiled=True),
        lax.all_gather(expert_gates, "ctx", axis=0, tiled=True),
    )
    all_ids = lax.all_gather(expert_ids, "ctx", axis=0, tiled=True)
    sources = all_tokens.shape[0] // moe_input.shape[0]
    per_source = moe_input.shape[0]
    token_grid = all_tokens.reshape(sources, per_source, all_tokens.shape[1])
    id_grid = all_ids.reshape(sources, per_source, all_ids.shape[1])
    gate_grid = all_gates.reshape(sources, per_source, all_gates.shape[1])

    def source_slots(id_rows, gate_rows, token_rows):
        table, _ = slot_table(id_rows, gate_rows, experts_here)
        return pick_rows(table, token_rows)

    all_slots = jax.vmap(source_slots)(id_grid, gate_grid, token_grid)
    all_slots = all_slots.reshape(sources * CAP, local_experts, all_tokens.shape[1])
    gate_val = jnp.einsum("red,edf->ref", all_slots, gate_proj, preferred_element_type=jnp.float32)
    up_val = jnp.einsum("red,edf->ref", all_slots, up_proj, preferred_element_type=jnp.float32)
    hidden = (jax.nn.silu(gate_val) * up_val).astype(jnp.bfloat16)
    terms = jnp.einsum("ref,efd->red", hidden, down_proj, preferred_element_type=jnp.float32)
    summed = lax.psum_scatter(
        terms.astype(jnp.bfloat16), "ctx", scatter_dimension=0, tiled=True
    ).astype(jnp.float32)
    coeff = onehot.astype(jnp.float32) * jnp.transpose(token_gate)[:, None, :]
    local_sum = jnp.einsum("ecm,ced->md", coeff, summed, precision=lax.Precision.HIGHEST)
    return lax.psum(local_sum.astype(jnp.bfloat16), "ep")


def per_device(
    lin_query,
    lin_keys,
    lin_values,
    log_decay,
    soft_query,
    soft_keys,
    soft_values,
    key_lists,
    moe_input,
    expert_ids,
    expert_gates,
    gate_proj,
    up_proj,
    down_proj,
):
    lin_mixed = lightning_part(lin_query, lin_keys, lin_values, log_decay)
    soft_mixed = softmax_part(soft_query, soft_keys, soft_values, key_lists)
    expert_mixed = expert_part(moe_input, expert_ids, expert_gates, gate_proj, up_proj, down_proj)
    return (lin_mixed, soft_mixed, expert_mixed)


def solution(mesh):
    placed = (
        P("ctx", "ep"),
        P("ctx", "ep"),
        P("ctx", "ep"),
        P("ctx", "ep"),
        P("ctx", "ep"),
        P("ctx", "ep"),
        P("ctx", "ep"),
        P("ctx", None),
        P("ctx", None),
        P("ctx", None),
        P("ctx", None),
        P("ep", None, "ctx"),
        P("ep", None, "ctx"),
        P("ep", "ctx", None),
    )
    return jax.shard_map(
        per_device,
        mesh=mesh,
        in_specs=placed,
        out_specs=(P("ctx", "ep"), P("ctx", "ep"), P("ctx", None)),
        check_vma=False,
    )
```

profile of v0, /device:TPU:1, one launch (start us, length us, event | category | flops | bytes accessed | tf_op | source)
XLA Modules:
  0.0 632.5 jit_solution(18424866565556648903)
XLA Ops:
  16.5 38.4 %all-gather.1 = bf16[32,1,4]{2,1,0:T(2,128)(2,1)} all-gather(bf16[1,1,4]{2,1,0:T(2,128)(2,1)S(1)} %bitcast.255), channel_id=1, replica_groups=mesh['ctx'=32,'ep'=8] {'ctx'}, dimensions={0}, use_global_device_ids=true | all-gather | bytes 264 | tf_op jit(solution)/shard_map/all_gather | solution.py:16
  56.5 35.5 %all-gather.2 = s32[32,16,2]{1,2,0:T(2,128)S(1)} all-gather(s32[1,16,2]{1,2,0:T(2,128)} %bitcast.251), channel_id=1, replica_groups=mesh['ctx'=32,'ep'=8] {'ctx'}, dimensions={0}, use_global_device_ids=true | all-gather | bytes 4224 | tf_op jit(solution)/shard_map/all_gather | solution.py:152
  109.3 3.9 fusion.26
  116.7 9.4 %fusion.27 = bf16[256,1,6144]{2,0,1:T(8,128)(2,1)} fusion(bf16[1,288,6144]{2,1,0:T(8,128)(2,1)S(1)} %copy-done, bf16[256,6144]{1,0:T(8,128)(2,1)} %copy-done.3, bf16[1,6144,288]{1,2,0:T(8,128)(2,1)} %param.30, f32[256,1,288]{0,2,1:T(8,128)} %fusion.37), kind=kOutput, calls=%fused_computation.45 | convolution fusion | flops 1813954560 | bytes 13664256 | tf_op jit(solution)/shard_map/ref,efd->red/dot_general | solution.py:168
  126.2 50.7 %all-gather.8.cloned.1.call-done = bf16[8192,128]{1,0:T(8,128)(2,1)} async-done(((bf16[256,128]{1,0:T(8,128)(2,1)}), bf16[8192,128]{1,0:T(8,128)(2,1)}) %all-gather.8.cloned.1.call-update) | async-done | bytes 2097168 | tf_op jit(solution)/shard_map/all_gather | solution.py:89
  176.9 77.7 %all-gather.10.cloned.1.call-done = bf16[8192,128]{1,0:T(8,128)(2,1)} async-done(((bf16[256,128]{1,0:T(8,128)(2,1)}), bf16[8192,128]{1,0:T(8,128)(2,1)}) %all-gather.10.cloned.1.call-update) | async-done | bytes 2097168 | tf_op jit(solution)/shard_map/all_gather | solution.py:90
  254.6 174.3 %while.30 = (s32[]{:T(128)}, f32[1,4,256]{2,1,0:T(4,128)S(1)}, f32[1,4,256]{2,1,0:T(4,128)S(1)}, f32[1,4,256,128]{3,2,1,0:T(8,128)}, s32[2,8]{1,0:T(2,128)S(1)},...) while((s32[]{:T(128)}, f32[1,4,256]{2,1,0:T(4,128)S(1)}, ...), condition=%wide.region_9.10_spmd.clone, body=%wide.region_5.9_spmd.clone.sunk | while | flops 275674112 | bytes 17636900 | solution.py:121
  272.1 3.5 fusion.118
  283.0 3.5 fusion.118
  293.9 3.5 fusion.118
  304.8 3.5 fusion.118
  315.7 3.6 fusion.118
  326.6 3.5 fusion.118
  337.6 3.5 fusion.118
  348.4 3.5 fusion.118
  359.3 3.5 fusion.118
  370.2 3.5 fusion.118
  381.1 3.5 fusion.118
  392.0 3.6 fusion.118
  403.0 3.5 fusion.118
  413.9 3.6 fusion.118
  424.8 3.5 fusion.118
  434.4 120.7 %reduce-scatter.2.cloned.1.call-done = bf16[8,1,6144]{2,0,1:T(8,128)(2,1)} async-done(((bf16[256,1,6144]{2,0,1:T(8,128)(2,1)}), bf16[8,1,6144]{2,0,1:T(8,128)(2,1)}) %reduce-scatter.2.cloned.1.call-update) | async-done | bytes 98320 | tf_op jit(solution)/shard_map/reduce_scatter | solution.py:169
  560.7 63.4 %all-reduce.2.cloned.1.call-done = bf16[16,6144]{1,0:T(8,128)(2,1)} async-done(((bf16[16,6144]{1,0:T(8,128)(2,1)}), bf16[16,6144]{1,0:T(8,128)(2,1)}) %all-reduce.2.cloned.1.call-update) | async-done | bytes 196624 | tf_op jit(solution)/shard_map/psum | solution.py:174
  (335 shorter events, 164.8 us)
Async XLA Ops:
  7.2 109.6 %copy-start = (bf16[1,288,6144]{2,1,0:T(8,128)(2,1)S(1)}, bf16[1,288,6144]{2,1,0:T(8,128)(2,1)}, u32[]{:S(2)}) copy-start(bf16[1,288,6144]{2,1,0:T(8,128)(2,1)} %param.31) | copy-start | bytes 10616836
  7.2 102.1 %all-gather.12.cloned.1.call-start = ((), (), s32[]{:S(2)}) async-start(), calls=%async_computation.3 | async-start | bytes 6488064 | tf_op jit(solution)/shard_map/all_gather | solution.py:149
  7.9 169.0 %all-gather.8.cloned.1.call-start = ((), (), s32[]{:S(2)}) async-start(), calls=%async_computation.1 | async-start | bytes 2162688 | tf_op jit(solution)/shard_map/all_gather | solution.py:89
  8.7 246.0 %all-gather.10.cloned.1.call-start = ((), (), s32[]{:S(2)}) async-start(), calls=%async_computation.2 | async-start | bytes 2162688 | tf_op jit(solution)/shard_map/all_gather | solution.py:90
  9.4 421.8 %all-gather.14.cloned.1.call-start = ((), (), s32[]{:S(2)}) async-start(), calls=%async_computation.6 | async-start | bytes 4325376 | tf_op jit(solution)/shard_map/all_gather | solution.py:16
  16.3 538.9 %reduce-scatter.2.cloned.1.call-start = ((), (), s32[]{:S(2)}) async-start(), calls=%async_computation.4 | async-start | bytes 3244032 | tf_op jit(solution)/shard_map/reduce_scatter | solution.py:169
  109.3 5.6 copy-start.9
  126.1 128.5 %copy-start.4 = (s32[2,8]{1,0:T(2,128)S(1)}, s32[2,8]{1,0:T(2,128)}, u32[]{:S(2)}) copy-start(s32[2,8]{1,0:T(2,128)} %param.25) | copy-start | bytes 196
  126.1 128.5 %copy-start.10 = (s32[16]{0:T(128)S(1)}, s32[16]{0:T(128)}, u32[]{:S(2)}) copy-start(s32[16]{0:T(128)} %iota_multiply_fusion) | copy-start | bytes 196
  126.1 497.9 %all-reduce.2.cloned.1.call-start = ((), (), s32[]{:S(2)}) async-start(), calls=%async_computation.5 | async-start | bytes 393216 | tf_op jit(solution)/shard_map/psum | solution.py:174
  315.7 3.6 copy-start.1
  315.7 3.6 copy-start.2
  326.6 3.6 copy-start.1
  326.6 3.6 copy-start.2
  359.3 3.6 copy-start.1
  370.2 3.6 copy-start.1
  392.0 3.6 copy-start.1
  392.0 3.6 copy-start.2
  402.9 3.6 copy-start.1
  413.9 3.6 copy-start.1
  413.9 3.6 copy-start.2
  431.9 123.3 %copy-start.6 = (f32[16]{0:T(128)S(1)}, f32[16]{0:T(128)}, u32[]{:S(2)}) copy-start(f32[16]{0:T(128)} %select_reduce_fusion) | copy-start | bytes 196
  431.9 123.3 %copy-start.7 = (s32[16]{0:T(128)S(1)}, s32[16]{0:T(128)}, u32[]{:S(2)}) copy-start(s32[16]{0:T(128)} %add_reduce_fusion) | copy-start | bytes 196
  431.9 123.3 %copy-start.8 = (pred[16]{0:T(512)(128)(4,1)S(1)}, pred[16]{0:T(512)(128)(4,1)}, u32[]{:S(2)}) copy-start(pred[16]{0:T(512)(128)(4,1)} %get-tuple-element.324) | copy-start | bytes 52
  (39 other events, 87.8 us)
Sparse Core Ops, SparseCore 0:
  10.6 92.1 all-gather.11
  105.4 71.4 all-gather.7
  179.5 75.1 all-gather.9
  257.6 80.2 all-gather.13
  341.7 213.4 reduce-scatter.1
  558.0 66.0 all-reduce.1
where the time goes:
time: 637 us; the launch traced here: 633 us
  waiting for transfers between devices  315 us (49%)
  matrix products  127 us (20%)
  blocking collectives  73.9 us (12%)
  local copies, waits for them, and re-layouts  66.1 us (10%)
  other arithmetic  35.8 us (6%)
  between operations  14.2 us (2%)
    reduce_scatter x1, waiting for transfers between devices, expert_part(): lax.psum_scatter(terms.astype(jnp.bfloat16), 'ctx', scatter_dimension=0,...  121 us
    all_gather x1, waiting for transfers between devices, softmax_part(): value_piece = lax.all_gather(soft_values, 'ctx', axis=0, tiled=True)  77.7 us
    psum x1, waiting for transfers between devices, expert_part(): return lax.psum(local_sum.astype(jnp.bfloat16), 'ep')  63.4 us
    dot_general x16, matrix products, visit(): jnp.einsum('kgts,skd->kgtd', weights.astype(jnp.bfloat16), value_block, p...  56.6 us
    all_gather x1, waiting for transfers between devices, softmax_part(): key_piece = lax.all_gather(soft_keys, 'ctx', axis=0, tiled=True)  50.7 us
    dot_general x16, matrix products, visit(): jnp.einsum('tkgd,skd->kgts', query_grid, key_block, preferred_element_typ...  46.2 us
    all_gather x1, blocking collectives, carried_in_2(): lax.all_gather(a.astype(kind), axis)  38.4 us
    all_gather x1, blocking collectives, expert_part(): all_ids = lax.all_gather(expert_ids, 'ctx', axis=0, tiled=True)  35.5 us
  transfers between devices with their start and end apart: 6, of which 4 were waited for; matrix products, arithmetic and copies ran while one was open for 35% of the time, Pallas kernels for 0%

commit v1 on v0

v1 whole, which is shorter than its diff:
```python
import functools

import jax
import jax.numpy as jnp
from jax import lax
from jax.experimental import pallas as pl
from jax.experimental.pallas import tpu as pltpu
from jax.sharding import PartitionSpec as P

HD = 128
BLK = 128
CAP = 8
F32 = jnp.float32
BF16 = jnp.bfloat16
VMEM = pl.BlockSpec(memory_space=pltpu.VMEM)
SMEM = pl.BlockSpec(memory_space=pltpu.SMEM)
PARAMS = pltpu.CompilerParams(vmem_limit_bytes=48 << 20)


def dot(a, b, dims=((1,), (0,)), precision=None):
    return lax.dot_general(a, b, (dims, ((), ())), precision=precision, preferred_element_type=F32)


def lower_ones(rows):
    at_row = lax.broadcasted_iota(jnp.int32, (rows, rows), 0)
    at_col = lax.broadcasted_iota(jnp.int32, (rows, rows), 1)
    return at_row >= at_col


def lightning_inside(query_ref, key_ref, value_ref, decay_ref, inside_ref, cumul_ref, send_ref):
    rows, heads = decay_ref.shape
    pieces = send_ref.shape[0] // heads
    depth = HD // pieces
    causal = lower_ones(rows)
    ones = causal.astype(F32)
    decay = decay_ref[...]
    cumul = dot(ones, decay, precision=lax.Precision.HIGHEST)
    cumul_rows = dot(decay, ones, ((0,), (1,)), lax.Precision.HIGHEST)
    cumul_ref[...] = cumul
    for h in range(heads):
        cols = slice(h * HD, (h + 1) * HD)
        query, key, value = query_ref[:, cols], key_ref[:, cols], value_ref[:, cols]
        along = cumul[:, h : h + 1]
        ending = cumul[rows - 1 : rows, h : h + 1]
        spread = along - cumul_rows[h : h + 1, :]
        weight = jnp.where(causal, jnp.exp(jnp.where(causal, spread, 0.0)), 0.0)
        scores = dot(query, key, ((1,), (1,))) * weight
        inside_ref[:, cols] = dot(scores.astype(BF16), value)
        carried = (jnp.exp(ending - along) * key.astype(F32)).astype(BF16)
        state = dot(carried, value, ((0,), (0,)))
        send_ref[h * pieces : (h + 1) * pieces, :depth, :] = state.astype(BF16).reshape(
            pieces, depth, HD
        )
        whole = jnp.broadcast_to(jnp.exp(ending), (depth, HD))
        first = whole.astype(BF16)
        rest = whole - first.astype(F32)
        second = rest.astype(BF16)
        third = (rest - second.astype(F32)).astype(BF16)
        place = lax.broadcasted_iota(jnp.int32, (depth, HD), 0)
        terms = jnp.where(
            place == 0,
            first.astype(F32),
            jnp.where(place == 1, second.astype(F32), jnp.where(place == 2, third.astype(F32), 0.0)),
        ).astype(BF16)
        for p in range(pieces):
            send_ref[h * pieces + p, depth:, :] = terms


def lightning_chain(got_ref, back_ref):
    places, _, _ = got_ref.shape
    depth = back_ref.shape[1]
    state = jnp.zeros((depth, HD), F32)
    for i in range(places):
        back_ref[i] = state.astype(BF16)
        block = got_ref[i].astype(F32)
        tail = block[depth:]
        whole = tail[0:1] + tail[1:2] + tail[2:3]
        state = whole * state + block[:depth]


def lightning_finish(query_ref, inside_ref, cumul_ref, state_ref, out_ref):
    heads = cumul_ref.shape[1]
    state = state_ref[...].reshape(heads * HD, HD)
    for h in range(heads):
        cols = slice(h * HD, (h + 1) * HD)
        carried = dot(query_ref[:, cols], state[h * HD : (h + 1) * HD])
        raw = inside_ref[:, cols] + jnp.exp(cumul_ref[:, h : h + 1]) * carried
        scale = lax.rsqrt(jnp.mean(raw * raw, axis=-1, keepdims=True) + 1e-05)
        out_ref[:, cols] = (raw * scale).astype(BF16)


def lightning_part(lin_query, lin_keys, lin_values, log_decay, places):
    rows, heads = log_decay.shape
    depth = heads * HD // places
    inside, cumul, send = pl.pallas_call(
        lightning_inside,
        out_shape=(
            jax.ShapeDtypeStruct((rows, heads * HD), F32),
            jax.ShapeDtypeStruct((rows, heads), F32),
            jax.ShapeDtypeStruct((places, 2 * depth, HD), BF16),
        ),
        in_specs=[VMEM] * 4,
        out_specs=(VMEM,) * 3,
        compiler_params=PARAMS,
        name="lightning_inside",
    )(lin_query, lin_keys, lin_values, log_decay)
    got = lax.all_to_all(send, "ctx", 0, 0)
    back = pl.pallas_call(
        lightning_chain,
        out_shape=jax.ShapeDtypeStruct((places, depth, HD), BF16),
        in_specs=[VMEM],
        out_specs=VMEM,
        compiler_params=PARAMS,
        name="lightning_chain",
    )(got)
    state = lax.all_to_all(back, "ctx", 0, 0)
    return pl.pallas_call(
        lightning_finish,
        out_shape=jax.ShapeDtypeStruct((rows, heads * HD), BF16),
        in_specs=[VMEM] * 4,
        out_specs=VMEM,
        compiler_params=PARAMS,
        name="lightning_finish",
    )(lin_query, inside, cumul, state)


def sparse_attention(lists_ref, query_ref, pairs_ref, out_ref, keys_ref, values_ref):
    blocks, picks = lists_ref.shape
    groups = query_ref.shape[1] // HD
    scaling = float(HD) ** (-0.5)
    for b in range(blocks):
        for n in range(picks):
            start = pl.multiple_of(lists_ref[b, n] * BLK, BLK)
            keys_ref[n * BLK : (n + 1) * BLK, :] = pairs_ref[pl.ds(start, BLK), :HD]
            values_ref[n * BLK : (n + 1) * BLK, :] = pairs_ref[pl.ds(start, BLK), HD:]
        for g in range(groups):
            cols = slice(g * HD, (g + 1) * HD)
            query = query_ref[b * BLK : (b + 1) * BLK, cols]
            scores = dot(query, keys_ref[...], ((1,), (1,))) * scaling
            weights = jnp.exp(scores - jnp.max(scores, axis=-1, keepdims=True))
            denom = jnp.sum(weights, axis=-1, keepdims=True)
            mixed = dot(weights.astype(BF16), values_ref[...])
            out_ref[b * BLK : (b + 1) * BLK, cols] = (mixed / denom).astype(BF16)


def softmax_part(soft_query, pairs, key_lists):
    picks = key_lists.shape[1]
    return pl.pallas_call(
        sparse_attention,
        out_shape=jax.ShapeDtypeStruct(soft_query.shape, BF16),
        in_specs=[SMEM, VMEM, VMEM],
        out_specs=VMEM,
        scratch_shapes=[pltpu.VMEM((picks * BLK, HD), BF16)] * 2,
        compiler_params=PARAMS,
        name="sparse_attention",
    )(key_lists, soft_query, pairs)


def pick_tokens(expert_ref, ids_ref, token_ref, out_ref):
    rows = ids_ref.shape[0]
    ids = ids_ref[...]
    match = jnp.any(ids == expert_ref[0], axis=1, keepdims=True)
    counted = jnp.broadcast_to(match.astype(F32), (rows, CAP))
    place = dot(lower_ones(rows).astype(F32), counted)
    slot = lax.broadcasted_iota(jnp.int32, (rows, CAP), 1).astype(F32) + 1.0
    onehot = jnp.where(match & (place == slot), 1.0, 0.0).astype(BF16)
    out_ref[...] = dot(onehot, token_ref[...], ((0,), (0,))).astype(BF16)


def feed_forward(slots_ref, gate_ref, up_ref, down_ref, out_ref):
    slots = slots_ref[...]
    gate_val = dot(slots, gate_ref[0])
    up_val = dot(slots, up_ref[0])
    hidden = (gate_val / (1.0 + jnp.exp(-gate_val)) * up_val).astype(BF16)
    width = 512
    for n in range(out_ref.shape[1] // width):
        cols = slice(n * width, (n + 1) * width)
        out_ref[:, cols] = dot(hidden, down_ref[0, :, cols]).astype(BF16)


def combine(ids_ref, gates_ref, sums_ref, out_ref):
    rows = ids_ref.shape[0]
    slots = sums_ref.shape[0]
    ids, gates = ids_ref[...], gates_ref[...].astype(F32)
    lane = lax.broadcasted_iota(jnp.int32, (rows, slots), 1)
    expert = lane // CAP
    slot = (lane - expert * CAP).astype(F32) + 1.0
    routed = jnp.zeros((rows, slots), F32)
    weight = jnp.zeros((rows, slots), F32)
    for k in range(ids.shape[1]):
        match = ids[:, k : k + 1] == expert
        routed = routed + jnp.where(match, 1.0, 0.0)
        weight = weight + jnp.where(match, gates[:, k : k + 1], 0.0)
    place = dot(lower_ones(rows).astype(F32), routed)
    coeff = jnp.where((routed > 0.0) & (place == slot), weight, 0.0).astype(BF16)
    out_ref[...] = dot(coeff, sums_ref[...]).astype(BF16)


def pick_part(moe_input, expert_ids):
    expert = lax.axis_index("ep").astype(jnp.int32).reshape(1)
    return pl.pallas_call(
        pick_tokens,
        out_shape=jax.ShapeDtypeStruct((CAP, moe_input.shape[1]), BF16),
        in_specs=[SMEM, VMEM, VMEM],
        out_specs=VMEM,
        compiler_params=PARAMS,
        name="pick_tokens",
    )(expert, expert_ids, moe_input)


def expert_part(all_slots, expert_ids, expert_gates, gate_proj, up_proj, down_proj, places):
    slots, width = all_slots.shape
    terms = pl.pallas_call(
        feed_forward,
        out_shape=jax.ShapeDtypeStruct((slots, width), BF16),
        in_specs=[VMEM] * 4,
        out_specs=VMEM,
        compiler_params=PARAMS,
        name="feed_forward",
    )(all_slots, gate_proj, up_proj, down_proj)
    parts = lax.all_to_all(terms.reshape(places, CAP, width), "ctx", 0, 0)
    sums = jnp.sum(parts.astype(F32), axis=0).astype(BF16)
    all_sums = lax.all_gather(sums, "ep", axis=0, tiled=True)
    return pl.pallas_call(
        combine,
        out_shape=jax.ShapeDtypeStruct((expert_ids.shape[0], width), BF16),
        in_specs=[VMEM] * 3,
        out_specs=VMEM,
        compiler_params=PARAMS,
        name="combine",
    )(expert_ids, expert_gates, all_sums)


def per_device(
    places,
    lin_query,
    lin_keys,
    lin_values,
    log_decay,
    soft_query,
    soft_keys,
    soft_values,
    key_lists,
    moe_input,
    expert_ids,
    expert_gates,
    gate_proj,
    up_proj,
    down_proj,
):
    picked = pick_part(moe_input, expert_ids)
    picked, soft_keys, soft_values = lax.optimization_barrier((picked, soft_keys, soft_values))
    all_slots = lax.all_gather(picked, "ctx", axis=0, tiled=True)
    pairs = lax.all_gather(
        jnp.concatenate([soft_keys, soft_values], axis=1), "ctx", axis=0, tiled=True
    )
    lin_mixed = lightning_part(lin_query, lin_keys, lin_values, log_decay, places)
    expert_mixed = expert_part(
        all_slots, expert_ids, expert_gates, gate_proj, up_proj, down_proj, places
    )
    soft_mixed = softmax_part(soft_query, pairs, key_lists)
    return (lin_mixed, soft_mixed, expert_mixed)


def solution(mesh):
    placed = (
        P("ctx", "ep"),
        P("ctx", "ep"),
        P("ctx", "ep"),
        P("ctx", "ep"),
        P("ctx", "ep"),
        P("ctx", "ep"),
        P("ctx", "ep"),
        P("ctx", None),
        P("ctx", None),
        P("ctx", None),
        P("ctx", None),
        P("ep", None, "ctx"),
        P("ep", None, "ctx"),
        P("ep", "ctx", None),
    )
    return jax.shard_map(
        functools.partial(per_device, mesh.shape["ctx"]),
        mesh=mesh,
        in_specs=placed,
        out_specs=(P("ctx", "ep"), P("ctx", "ep"), P("ctx", None)),
        check_vma=False,
    )
```

time: 637 us -> 237 us (0.37)
  waiting for transfers between devices: 315 us -> 126 us
  matrix products: 127 us -> 0 us
  local copies, waits for them, and re-layouts: 66.1 us -> 20.3 us
  blocking collectives: 73.9 us -> 39.5 us
  other arithmetic: 35.8 us -> 3.87 us
  Pallas kernels: 0 us -> 22.3 us
  starting transfers between devices: 0.23 us -> 10.2 us
    dot_general x39 -> x0, matrix products: 127 us -> none  [the longest x16 56.6 us: visit(): jnp.einsum('kgts,skd->kgtd', weights.astype(jnp.bfloat16), value_block, p...]
    reduce_scatter x1 -> x0, waiting for transfers between devices: 121 us -> none  [expert_part(): lax.psum_scatter(terms.astype(jnp.bfloat16), 'ctx', scatter_dimension=0,...]
    psum x1 -> x0, waiting for transfers between devices: 63.4 us -> none  [expert_part(): return lax.psum(local_sum.astype(jnp.bfloat16), 'ep')]
    all_gather x2 -> x1, blocking collectives: 73.9 us -> 14.8 us  [expert_part(): all_sums = lax.all_gather(sums, 'ep', axis=0, tiled=True)]
    broadcast_in_dim x33 -> x0, local copies, waits for them, and re-layouts: 40.1 us -> none  [the longest x16 28.2 us: visit(): scores = jnp.where(allowed, scores, -1e+30)]
    all_to_all x0 -> x1, blocking collectives: none -> 24.7 us  [lightning_part(): got = lax.all_to_all(send, 'ctx', 0, 0)]
    pallas_call x0 -> x7, Pallas kernels: none -> 22.3 us  [the longest x1 12.4 us: expert_part(): pl.pallas_call(feed_forward, out_shape=jax.ShapeDtypeStruct((slots, width...]
    unnamed x24 -> x23, local copies, waits for them, and re-layouts: 9.47 us -> 20.3 us
  transfers between devices with their start and end apart: 6 -> 4, of which waited for: 4 -> 2; matrix products, arithmetic and copies ran while one was open for 35% -> 6% of each run, Pallas kernels for 0% -> 9%
where the time goes in v1:
time: 237 us; the launch traced here: 236 us
  waiting for transfers between devices  126 us (53%)
  blocking collectives  39.5 us (17%)
  Pallas kernels  22.3 us (9%)
  local copies, waits for them, and re-layouts  20.3 us (9%)
  between operations  14.1 us (6%)
  starting transfers between devices  10.2 us (4%)
  other arithmetic  3.87 us (2%)
    all_gather x1, waiting for transfers between devices, per_device(): lax.all_gather(jnp.concatenate([soft_keys, soft_values], axis=1), 'ctx',...  94 us
    all_gather x1, waiting for transfers between devices, per_device(): all_slots = lax.all_gather(picked, 'ctx', axis=0, tiled=True)  32.1 us
    all_to_all x1, blocking collectives, lightning_part(): got = lax.all_to_all(send, 'ctx', 0, 0)  24.7 us
    unnamed x23, local copies, waits for them, and re-layouts  20.3 us
    all_gather x1, blocking collectives, expert_part(): all_sums = lax.all_gather(sums, 'ep', axis=0, tiled=True)  14.8 us
    pallas_call x1, Pallas kernels, expert_part(): pl.pallas_call(feed_forward, out_shape=jax.ShapeDtypeStruct((slots, width...  12.4 us
    all_to_all x1, starting transfers between devices, expert_part(): parts = lax.all_to_all(terms.reshape(places, CAP, width), 'ctx', 0, 0)  5.8 us
  transfers between devices with their start and end apart: 4, of which 2 were waited for; matrix products, arithmetic and copies ran while one was open for 6% of the time, Pallas kernels for 9%

profile of v1, /device:TPU:1, one launch (start us, length us, event | category | flops | bytes accessed | tf_op | source)
XLA Modules:
  0.0 236.4 jit_solution(4751989100783478174)
XLA Ops:
  7.2 0.8 copy.18.ids_ref
  8.0 0.9 copy-done.6
  8.9 1.1 pick_tokens.1
  10.0 1.5 pad_maximum_fusion
  11.6 0.8 copy.17.decay_ref
  12.4 0.9 copy-done.1
  13.4 0.9 copy-done.3
  14.3 0.9 copy-done.4
  15.3 1.4 lightning_inside.1
  16.7 24.7 %all_to_all.15.got_ref = bf16[32,32,128]{2,1,0:T(8,128)(2,1)S(1)} all-to-all(bf16[32,32,128]{2,1,0:T(8,128)(2,1)S(1)} %get-tuple-element.11), channel_id=1, replica_groups=mesh['ctx'=32,'ep'=8] {'ctx'}, dimensions={0} | all-to-all | bytes 524288 | tf_op jit(solution)/shard_map/all_to_all | solution.py:107
  41.3 0.7 lightning_chain.1
  42.0 4.3 %all-to-all-start.1 = ((bf16[32,16,128]{2,1,0:T(8,128)(2,1)}), bf16[32,16,128]{2,1,0:T(8,128)(2,1)S(1)}, u32[]{:S(2)}, u32[]{:S(2)}) async-start(bf16[32,16,128]{2,1,0:T(8,128)(2,1)} %lightning_chain.1), calls=%async_computation.1 | async-start | bytes 262144 | tf_op jit(solution)/shard_map/all_to_all | solution.py:116
  46.4 6.3 %copy.19.gate_ref = bf16[1,6144,288]{2,1,0:T(8,128)(2,1)} copy(bf16[1,6144,288]{1,2,0:T(8,128)(2,1)} %param.25) | data formatting | bytes 7077888 | tf_op args[11]
  52.6 6.3 %copy.20.up_ref = bf16[1,6144,288]{2,1,0:T(8,128)(2,1)} copy(bf16[1,6144,288]{1,2,0:T(8,128)(2,1)} %param.26) | data formatting | bytes 7077888 | tf_op args[12]
  59.0 32.1 %all-gather.5.cloned.1.call-done.slots_ref = bf16[256,6144]{1,0:T(8,128)(2,1)} async-done(((bf16[8,6144]{1,0:T(8,128)(2,1)}), bf16[256,6144]{1,0:T(8,128)(2,1)}) %all-gather.5.cloned.1.call-update) | async-done | bytes 3145744 | tf_op jit(solution)/shard_map/all_gather | solution.py:253
  91.0 12.4 %feed_forward.1 = bf16[256,6144]{1,0:T(8,128)(2,1)} custom-call(bf16[256,6144]{1,0:T(8,128)(2,1)} %all-gather.5.cloned.1.call-done.slots_ref, bf16[1,6144,288]{2,1,0:T(8,128)(2,1)} %copy.19.gate_ref, bf16[1,6144,288]{2,1,0:T(8,128)(2,1)} %copy.20.up_ref, bf16[1,288,6144]{2,1,0:T(8,128)(2,1)} %down_ref.1), custom_call_target="tpu_custom_call" | custom-call | tf_op jit(solution)/shard_map/feed_forward/pallas_call | solution.py:213
  103.5 5.8 %all-to-all-start.2 = ((bf16[32,8,6144]{2,1,0:T(8,128)(2,1)}), bf16[32,8,6144]{2,1,0:T(8,128)(2,1)}, u32[]{:S(2)}, u32[]{:S(2)}) async-start(bf16[32,8,6144]{2,1,0:T(8,128)(2,1)} %bitcast.1), calls=%async_computation.2 | async-start | bytes 6291456 | tf_op jit(solution)/shard_map/all_to_all | solution.py:221
  109.4 1.3 lightning_finish.1
  110.7 94.0 %all-gather.3.cloned.1.call-done.pairs_ref = bf16[8192,256]{1,0:T(8,128)(2,1)} async-done(((bf16[256,256]{1,0:T(8,128)(2,1)}), bf16[8192,256]{1,0:T(8,128)(2,1)}) %all-gather.3.cloned.1.call-update) | async-done | bytes 4194320 | tf_op jit(solution)/shard_map/all_gather | solution.py:254
  204.7 2.2 copy-done
  206.9 4.3 %sparse_attention.1 = bf16[256,512]{1,0:T(8,128)(2,1)} custom-call(s32[2,8]{1,0:T(2,128)S(1)} %copy-done.7, bf16[256,512]{1,0:T(8,128)(2,1)S(1)} %copy-done.5, bf16[8192,256]{1,0:T(8,128)(2,1)S(1)} %copy-done), custom_call_target="tpu_custom_call" | custom-call | tf_op jit(solution)/shard_map/sparse_attention/pallas_call | solution.py:148
  211.3 2.3 reduce_sum.12
  213.6 14.8 %all_gather.11.sums_ref = bf16[64,6144]{1,0:T(8,128)(2,1)S(1)} all-gather(bf16[8,6144]{1,0:T(8,128)(2,1)S(1)} %reduce_sum.12), channel_id=1, replica_groups=mesh['ctx'=32,'ep'=8] {'ep'}, dimensions={0}, use_global_device_ids=true | all-gather | bytes 884736 | tf_op jit(solution)/shard_map/all_gather | solution.py:223
  228.4 1.1 combine.1
  (20 shorter events, 0.2 us)
Async XLA Ops:
  7.2 83.9 %all-gather.5.cloned.1.call-start = ((), (), s32[]{:S(2)}) async-start(), calls=%async_computation.4 | async-start | bytes 3244032 | tf_op jit(solution)/shard_map/all_gather | solution.py:253
  8.0 0.9 copy-start.6
  10.0 194.7 %all-gather.3.cloned.1.call-start = ((), (), s32[]{:S(2)}) async-start(), calls=%async_computation.3 | async-start | bytes 4325376 | tf_op jit(solution)/shard_map/all_gather | solution.py:254
  12.4 1.0 copy-start.1
  13.4 0.9 copy-start.3
  14.3 0.9 copy-start.4
  42.0 61.5 %all-to-all-start.1 = ((bf16[32,16,128]{2,1,0:T(8,128)(2,1)}), bf16[32,16,128]{2,1,0:T(8,128)(2,1)S(1)}, u32[]{:S(2)}, u32[]{:S(2)}) async-start(bf16[32,16,128]{2,1,0:T(8,128)(2,1)} %lightning_chain.1), calls=%async_computation.1 | async-start | bytes 262144 | tf_op jit(solution)/shard_map/all_to_all | solution.py:116
  103.5 5.8 %copy-start.8 = (bf16[16,2]{0,1:T(2,128)(2,1)S(1)}, bf16[16,2]{0,1:T(2,128)(2,1)}, u32[]{:S(2)}) copy-start(bf16[16,2]{0,1:T(2,128)(2,1)} %param.24) | copy-start | bytes 196
  103.5 5.9 %copy-start.2 = (bf16[256,512]{1,0:T(8,128)(2,1)S(1)}, bf16[256,512]{1,0:T(8,128)(2,1)}, u32[]{:S(2)}) copy-start(bf16[256,512]{1,0:T(8,128)(2,1)} %query_ref.4) | copy-start | bytes 786436
  103.5 101.2 %copy-start.5 = (bf16[256,512]{1,0:T(8,128)(2,1)S(1)}, bf16[256,512]{1,0:T(8,128)(2,1)}, u32[]{:S(2)}) copy-start(bf16[256,512]{1,0:T(8,128)(2,1)} %query_ref.5) | copy-start | bytes 786436
  103.5 101.2 %copy-start.7 = (s32[2,8]{1,0:T(2,128)S(1)}, s32[2,8]{1,0:T(2,128)}, u32[]{:S(2)}) copy-start(s32[2,8]{1,0:T(2,128)} %lists_ref.1) | copy-start | bytes 196
  103.5 107.7 %all-to-all-start.2 = ((bf16[32,8,6144]{2,1,0:T(8,128)(2,1)}), bf16[32,8,6144]{2,1,0:T(8,128)(2,1)}, u32[]{:S(2)}, u32[]{:S(2)}) async-start(bf16[32,8,6144]{2,1,0:T(8,128)(2,1)} %bitcast.1), calls=%async_computation.2 | async-start | bytes 6291456 | tf_op jit(solution)/shard_map/all_to_all | solution.py:221
  204.7 2.2 copy-start
Sparse Core Ops, SparseCore 0:
  11.2 79.8 all-gather.4
  94.2 110.4 all-gather.2

commit v2 on v1

v2 whole, which is shorter than its diff:
```python
import functools

import jax
import jax.numpy as jnp
from jax import lax
from jax.experimental import pallas as pl
from jax.experimental.pallas import tpu as pltpu
from jax.sharding import Mesh
from jax.sharding import PartitionSpec as P

HD = 128
BLK = 128
CAP = 8
F32 = jnp.float32
BF16 = jnp.bfloat16
VMEM = pl.BlockSpec(memory_space=pltpu.VMEM)
SMEM = pl.BlockSpec(memory_space=pltpu.SMEM)
ANY = pl.BlockSpec(memory_space=pl.ANY)
PARAMS = pltpu.CompilerParams(vmem_limit_bytes=16 << 20)
X = 4
CTX = ("z", "x")
CHUNKS = 6


def dot(a, b, dims=((1,), (0,)), precision=None):
    return lax.dot_general(a, b, (dims, ((), ())), precision=precision, preferred_element_type=F32)


def called(kernel, out_shape, operands, specs, after=(), scratch=(), limit=16, cost=None, name=None):
    given = len(operands)

    def body(*refs):
        kernel(*refs[:given], *refs[given + len(after) :])

    many = isinstance(out_shape, tuple)
    return pl.pallas_call(
        body,
        out_shape=out_shape,
        in_specs=list(specs) + [ANY] * len(after),
        out_specs=(VMEM,) * len(out_shape) if many else VMEM,
        scratch_shapes=scratch,
        compiler_params=pltpu.CompilerParams(vmem_limit_bytes=limit << 20),
        cost_estimate=cost,
        name=name,
    )(*operands, *after)


def lower_ones(rows):
    at_row = lax.broadcasted_iota(jnp.int32, (rows, rows), 0)
    at_col = lax.broadcasted_iota(jnp.int32, (rows, rows), 1)
    return at_row >= at_col


def lightning_inside(query_ref, key_ref, value_ref, decay_ref, inside_ref, cumul_ref, send_ref):
    heads, rows = decay_ref.shape
    pieces = send_ref.shape[0] // heads
    depth = HD // pieces
    causal = lower_ones(rows)
    ones = causal.astype(F32)
    decay = decay_ref[...]
    cumul = dot(ones, decay, ((1,), (1,)), lax.Precision.HIGHEST)
    cumul_rows = dot(decay, ones, ((1,), (1,)), lax.Precision.HIGHEST)
    cumul_ref[...] = cumul
    for h in range(heads):
        cols = slice(h * HD, (h + 1) * HD)
        query, key, value = query_ref[:, cols], key_ref[:, cols], value_ref[:, cols]
        along = cumul[:, h : h + 1]
        ending = cumul[rows - 1 : rows, h : h + 1]
        spread = along - cumul_rows[h : h + 1, :]
        weight = jnp.where(causal, jnp.exp(jnp.where(causal, spread, 0.0)), 0.0)
        scores = dot(query, key, ((1,), (1,))) * weight
        inside_ref[:, cols] = dot(scores.astype(BF16), value)
        carried = (jnp.exp(ending - along) * key.astype(F32)).astype(BF16)
        state = dot(carried, value, ((0,), (0,)))
        send_ref[h * pieces : (h + 1) * pieces, :depth, :] = state.astype(BF16).reshape(
            pieces, depth, HD
        )
        whole = jnp.broadcast_to(jnp.exp(ending), (depth, HD))
        first = whole.astype(BF16)
        rest = whole - first.astype(F32)
        second = rest.astype(BF16)
        third = (rest - second.astype(F32)).astype(BF16)
        place = lax.broadcasted_iota(jnp.int32, (depth, HD), 0)
        terms = jnp.where(
            place == 0,
            first.astype(F32),
            jnp.where(place == 1, second.astype(F32), jnp.where(place == 2, third.astype(F32), 0.0)),
        ).astype(BF16)
        for p in range(pieces):
            send_ref[h * pieces + p, depth:, :] = terms


def lightning_chain(got_ref, back_ref):
    places, _, _ = got_ref.shape
    depth = back_ref.shape[1]
    state = jnp.zeros((depth, HD), F32)
    for i in range(places):
        back_ref[i] = state.astype(BF16)
        block = got_ref[i].astype(F32)
        tail = block[depth:]
        whole = tail[0:1] + tail[1:2] + tail[2:3]
        state = whole * state + block[:depth]


def lightning_finish(query_ref, inside_ref, cumul_ref, state_ref, out_ref):
    heads = cumul_ref.shape[1]
    state = state_ref[...].reshape(heads * HD, HD)
    for h in range(heads):
        cols = slice(h * HD, (h + 1) * HD)
        carried = dot(query_ref[:, cols], state[h * HD : (h + 1) * HD])
        raw = inside_ref[:, cols] + jnp.exp(cumul_ref[:, h : h + 1]) * carried
        scale = lax.rsqrt(jnp.mean(raw * raw, axis=-1, keepdims=True) + 1e-05)
        out_ref[:, cols] = (raw * scale).astype(BF16)


def lightning_begin(lin_query, lin_keys, lin_values, log_decay, after):
    rows, heads = log_decay.shape
    places = lax.axis_size(CTX)
    return called(
        lightning_inside,
        (
            jax.ShapeDtypeStruct((rows, heads * HD), F32),
            jax.ShapeDtypeStruct((rows, heads), F32),
            jax.ShapeDtypeStruct((places, 2 * heads * HD // places, HD), BF16),
        ),
        (lin_query, lin_keys, lin_values, log_decay.T),
        [VMEM] * 4,
        after,
        name="lightning_inside",
    )


def lightning_states(got, after):
    places, rows, _ = got.shape
    out_shape = jax.ShapeDtypeStruct((places, rows // 2, HD), BF16)
    return called(lightning_chain, out_shape, (got,), [VMEM], after, name="lightning_chain")


def lightning_end(lin_query, inside, cumul, state, after):
    out_shape = jax.ShapeDtypeStruct(lin_query.shape, BF16)
    operands = (lin_query, inside, cumul, state)
    return called(lightning_finish, out_shape, operands, [VMEM] * 4, after, name="lightning_finish")


def sparse_attention(lists_ref, query_ref, pairs_ref, out_ref, keys_ref, values_ref):
    blocks, picks = lists_ref.shape
    groups = query_ref.shape[1] // HD
    scaling = float(HD) ** (-0.5)
    for b in range(blocks):
        for n in range(picks):
            start = pl.multiple_of(lists_ref[b, n] * BLK, BLK)
            keys_ref[n * BLK : (n + 1) * BLK, :] = pairs_ref[pl.ds(start, BLK), :HD]
            values_ref[n * BLK : (n + 1) * BLK, :] = pairs_ref[pl.ds(start, BLK), HD:]
        for g in range(groups):
            cols = slice(g * HD, (g + 1) * HD)
            query = query_ref[b * BLK : (b + 1) * BLK, cols]
            scores = dot(query, keys_ref[...], ((1,), (1,))) * scaling
            weights = jnp.exp(scores - jnp.max(scores, axis=-1, keepdims=True))
            denom = jnp.sum(weights, axis=-1, keepdims=True)
            mixed = dot(weights.astype(BF16), values_ref[...])
            out_ref[b * BLK : (b + 1) * BLK, cols] = (mixed / denom).astype(BF16)


def softmax_part(soft_query, pairs, key_lists, after):
    picks = key_lists.shape[1]
    return called(
        sparse_attention,
        jax.ShapeDtypeStruct(soft_query.shape, BF16),
        (key_lists, soft_query, pairs),
        [SMEM, VMEM, VMEM],
        after,
        [pltpu.VMEM((picks * BLK, HD), BF16)] * 2,
        name="sparse_attention",
    )


def shift(a, axis, by):
    size = lax.axis_size(axis)
    return lax.ppermute(a, axis, [(i, (i + by) % size) for i in range(size)])


def pick_tokens(expert_ref, ids_ref, token_ref, out_ref):
    top, rows = ids_ref.shape
    match = jnp.zeros((1, rows), F32)
    for k in range(top):
        match = match + jnp.where(ids_ref[k : k + 1, :] == expert_ref[0], 1.0, 0.0)
    match = jnp.broadcast_to(match, (CAP, rows))
    place = dot(match, lower_ones(rows).astype(F32), ((1,), (1,)))
    slot = lax.broadcasted_iota(jnp.int32, (CAP, rows), 0).astype(F32) + 1.0
    onehot = jnp.where((match > 0.0) & (place == slot), 1.0, 0.0).astype(BF16)
    out_ref[...] = dot(onehot, token_ref[...]).astype(BF16)


def feed_forward(pieces, *refs):
    gate_ref, up_ref, down_ref = refs[pieces : pieces + 3]
    leaving_refs = refs[pieces + 3 :]
    slots = jnp.concatenate([ref[...] for ref in refs[:pieces]], axis=0)
    gate_val = dot(slots, gate_ref[0], ((1,), (1,)))
    up_val = dot(slots, up_ref[0], ((1,), (1,)))
    hidden = (gate_val / (1.0 + jnp.exp(-gate_val)) * up_val).astype(BF16)
    span = X * CAP
    full = down_ref.shape[2]
    width = full // CHUNKS
    for n in range(CHUNKS):
        terms = dot(hidden, down_ref[0, :, n * width : (n + 1) * width])
        parts = []
        for k in range(X):
            rows = [terms[at + k * CAP : at + (k + 1) * CAP] for at in range(0, terms.shape[0], span)]
            parts.append(jnp.concatenate(rows, axis=0).astype(BF16))
        side = n // (CHUNKS // 2)
        at = n * width - side * (full // 2)
        ways = (0, 2, 3, 1) if side == 0 else (0, 1, 2, 3)
        for ref, k in zip(leaving_refs[4 * side : 4 * side + 4], ways, strict=True):
            ref[:, at : at + width] = parts[k]


def load(*refs):
    sems = refs[-1]
    copies = [pltpu.make_async_copy(refs[n], refs[n + 3], sems.at[n]) for n in range(3)]
    for copy in copies:
        copy.start()
    for copy in copies:
        copy.wait()


def loaded(weights, after):
    out_shape = tuple(jax.ShapeDtypeStruct(w.shape, BF16) for w in weights)
    sems = [pltpu.SemaphoreType.DMA((3,))]
    return called(load, out_shape, weights, [ANY] * 3, after, sems, name="load")


def relay(own_ref, came_ref, out_ref):
    out_ref[...] = (own_ref[...].astype(F32) + came_ref[...].astype(F32)).astype(BF16)


def add_parts(z_ref, *refs):
    out_ref = refs[-1]
    many = out_ref.shape[0]
    half = refs[0].shape[1]
    for side in range(2):
        here, direct, relayed = (ref[...].astype(F32) for ref in refs[3 * side : 3 * side + 3])
        total = here + direct + relayed
        cols = slice(side * half, (side + 1) * half)
        for m in range(many):
            away = (m + 1) // 2 if m % 2 == 0 else -((m + 1) // 2)
            place = lax.rem(z_ref[0] + away + many, many)
            out_ref[place, :, cols] = total[m * CAP : (m + 1) * CAP].astype(BF16)


def add_all(parts_ref, out_ref):
    total = parts_ref[0].astype(F32)
    for n in range(1, parts_ref.shape[0]):
        total = total + parts_ref[n].astype(F32)
    out_ref[...] = total.astype(BF16)


def stack(*refs):
    rows = [ref[...].astype(F32) for ref in refs[:-1]]
    refs[-1][...] = jnp.concatenate(rows, axis=0).astype(BF16)


def combine(expert_ref, ids_ref, gates_ref, mine_ref, other_ref, out_ref):
    rows = ids_ref.shape[0]
    slots = mine_ref.shape[0]
    turns = slots // CAP
    ids, gates = ids_ref[...], gates_ref[...].astype(F32)
    lane = lax.broadcasted_iota(jnp.int32, (rows, slots), 1)
    block = lane // CAP
    slot = (lane - block * CAP).astype(F32) + 1.0
    ones = lower_ones(rows).astype(F32)
    y, core = expert_ref[0] // 2, lax.rem(expert_ref[0], 2)
    total = jnp.zeros(out_ref.shape, F32)
    for swap, sums_ref in enumerate((mine_ref, other_ref)):
        expert = lax.rem(y - block + turns, turns) * 2 + (core + swap - 2 * core * swap)
        routed = jnp.zeros((rows, slots), F32)
        weight = jnp.zeros((rows, slots), F32)
        for k in range(ids.shape[1]):
            match = ids[:, k : k + 1] == expert
            routed = routed + jnp.where(match, 1.0, 0.0)
            weight = weight + jnp.where(match, gates[:, k : k + 1], 0.0)
        place = dot(ones, routed)
        coeff = jnp.where((routed > 0.0) & (place == slot), weight, 0.0).astype(BF16)
        total = total + dot(coeff, sums_ref[...])
    out_ref[...] = total.astype(BF16)


def pick_part(moe_input, expert_ids):
    expert = lax.axis_index("ep").astype(jnp.int32).reshape(1)
    return pl.pallas_call(
        pick_tokens,
        out_shape=jax.ShapeDtypeStruct((CAP, moe_input.shape[1]), BF16),
        in_specs=[SMEM, VMEM, VMEM],
        out_specs=VMEM,
        compiler_params=PARAMS,
        name="pick_tokens",
    )(expert, expert_ids.T, moe_input)


def expert_part(
    picked, expert_ids, expert_gates, gate_proj, up_proj, down_proj, begin, states, finish, attend
):
    width = picked.shape[1]
    weights = (jnp.swapaxes(gate_proj, 1, 2), jnp.swapaxes(up_proj, 1, 2), down_proj)
    hidden = down_proj.shape[1]

    inside, cumul, send = begin(())
    own = called(
        stack,
        jax.ShapeDtypeStruct((X * CAP, width), BF16),
        (picked, *(shift(picked, "x", k) for k in range(1, X))),
        [VMEM] * X,
        (send,),
        name="stack",
    )
    half = X * CAP // 2
    ahead1, back1 = shift(own, "z", 1), shift(own, "z", -1)
    got = lax.all_to_all(send, CTX, 0, 0)
    ahead2, back2 = shift(ahead1, "z", 1), shift(back1, "z", -1)
    spread = states(got, (ahead2, back2))
    ahead3, back3 = shift(ahead2, "z", 1), shift(back2, "z", -1)
    weights = loaded(weights, (ahead3, back3))
    far = [shift(ahead3[:half], "z", 1), shift(back3[half:], "z", -1)]
    blocks = [own, ahead1, back1, ahead2, back2, ahead3, back3] + far
    rows = sum(block.shape[0] for block in blocks)
    part = jax.ShapeDtypeStruct((rows // X, width // 2), BF16)
    leaving = called(
        functools.partial(feed_forward, len(blocks)),
        (part,) * 8,
        (*blocks, *weights),
        [VMEM] * (len(blocks) + 3),
        (spread,),
        (),
        24,
        pl.CostEstimate(
            flops=6 * rows * width * hidden,
            bytes_accessed=6 * width * hidden + 4 * rows * width,
            transcendentals=rows * hidden,
        ),
        "feed_forward",
    )
    state = lax.all_to_all(spread, CTX, 0, 0)
    parts = []
    for side in range(2):
        here, minus, plus, mine = leaving[4 * side : 4 * side + 4]
        minus, plus = shift(minus, "x", -1), shift(plus, "x", 1)
        came, direct = (minus, plus) if side == 0 else (plus, minus)
        relayed = called(relay, part, (mine, came), [VMEM] * 2, name="relay")
        parts += [here, direct, shift(relayed, "x", -1 if side == 0 else 1)]
    many = rows // X // CAP
    sums = called(
        add_parts,
        jax.ShapeDtypeStruct((many, CAP, width), BF16),
        (lax.axis_index("z").astype(jnp.int32).reshape(1), *parts),
        [SMEM] + [VMEM] * 6,
        (state,),
        name="add_parts",
    )
    lin_mixed = finish(inside, cumul, state, (sums,))
    soft_mixed = attend((sums,))
    sums = lax.all_to_all(sums, "z", 0, 0)
    total = called(
        add_all,
        jax.ShapeDtypeStruct((CAP, width), BF16),
        (sums,),
        [VMEM],
        (soft_mixed, lin_mixed),
        name="add_all",
    )
    experts = lax.axis_size("ep")
    blocks = [total]
    for k in range(1, experts // 2):
        pairs_of = [(i, (i + 2 * k) % experts) for i in range(experts)]
        blocks.append(lax.ppermute(total, "ep", pairs_of))
    mine = called(
        stack,
        jax.ShapeDtypeStruct((len(blocks) * CAP, width), BF16),
        tuple(blocks),
        [VMEM] * len(blocks),
        name="stack",
    )
    other = lax.ppermute(mine, "ep", [(i, i ^ 1) for i in range(experts)])
    expert = lax.axis_index("ep").astype(jnp.int32).reshape(1)
    mixed = called(
        combine,
        jax.ShapeDtypeStruct((expert_ids.shape[0], width), BF16),
        (expert, expert_ids, expert_gates, mine, other),
        [SMEM] + [VMEM] * 4,
        name="combine",
    )
    return mixed, (lin_mixed, soft_mixed)


def per_device(
    lin_query,
    lin_keys,
    lin_values,
    log_decay,
    soft_query,
    soft_keys,
    soft_values,
    key_lists,
    moe_input,
    expert_ids,
    expert_gates,
    gate_proj,
    up_proj,
    down_proj,
):
    picked = pick_part(moe_input, expert_ids)
    picked, soft_keys, soft_values = lax.optimization_barrier((picked, soft_keys, soft_values))
    pairs = lax.all_gather(
        jnp.concatenate([soft_keys, soft_values], axis=1), CTX, axis=0, tiled=True
    )
    begin = functools.partial(lightning_begin, lin_query, lin_keys, lin_values, log_decay)
    finish = functools.partial(lightning_end, lin_query)
    attend = functools.partial(softmax_part, soft_query, pairs, key_lists)
    expert_mixed, (lin_mixed, soft_mixed) = expert_part(
        picked,
        expert_ids,
        expert_gates,
        gate_proj,
        up_proj,
        down_proj,
        begin,
        lightning_states,
        finish,
        attend,
    )
    return (lin_mixed, soft_mixed, expert_mixed)


def solution(mesh):
    places, experts = mesh.devices.shape
    fine = Mesh(mesh.devices.reshape(places // X, X, experts), CTX + ("ep",))
    both, rows = P(CTX, "ep"), P(CTX, None)
    placed = (both,) * 7 + (rows,) * 4 + (P("ep", None, CTX),) * 2 + (P("ep", CTX, None),)
    return jax.shard_map(
        per_device,
        mesh=fine,
        in_specs=placed,
        out_specs=(both, both, rows),
        check_vma=False,
    )
```

time: 237 us -> 165 us (0.70)
  waiting for transfers between devices: 126 us -> 42.6 us
  starting transfers between devices: 10.2 us -> 63.5 us
  blocking collectives: 39.5 us -> 0 us
    all_gather x2 -> x1, waiting for transfers between devices: 126 us -> 0.01 us  [per_device(): lax.all_gather(jnp.concatenate([soft_keys, soft_values], axis=1), CTX, ax...]
    ppermute x0 -> x21, starting transfers between devices: none -> 45.6 us  [the longest x17 28.9 us: shift(): return lax.ppermute(a, axis, [(i, (i + by) % size) for i in range(size)])]
    all_to_all x1 -> x0, blocking collectives: 24.7 us -> none  [lightning_part(): got = lax.all_to_all(send, 'ctx', 0, 0)]
    ppermute x0 -> x21, waiting for transfers between devices: none -> 22.3 us  [the longest x17 19.5 us: shift(): return lax.ppermute(a, axis, [(i, (i + by) % size) for i in range(size)])]
    all_to_all x2 -> x3, waiting for transfers between devices: 0.01 us -> 20.3 us  [the longest x1 9.32 us: expert_part(): state = lax.all_to_all(spread, CTX, 0, 0)]
    all_gather x1 -> x0, blocking collectives: 14.8 us -> none  [expert_part(): all_sums = lax.all_gather(sums, 'ep', axis=0, tiled=True)]
    all_to_all x2 -> x3, starting transfers between devices: 10.1 us -> 17.8 us  [the longest x1 6.63 us: expert_part(): state = lax.all_to_all(spread, CTX, 0, 0)]
    slice x0 -> x2, local copies, waits for them, and re-layouts: none -> 3.23 us  [expert_part(): far = [shift(ahead3[:half], 'z', 1), shift(back3[half:], 'z', -1)]]
  transfers between devices with their start and end apart: 4 -> 25, of which waited for: 2 -> 11; matrix products, arithmetic and copies ran while one was open for 6% -> 2% of each run, Pallas kernels for 9% -> 12%
where the time goes in v2:
time: 165 us; the launch traced here: 164 us
  starting transfers between devices  63.5 us (38%)
  waiting for transfers between devices  42.6 us (26%)
  local copies, waits for them, and re-layouts  21.6 us (13%)
  Pallas kernels  20.5 us (12%)
  between operations  14.3 us (9%)
    ppermute x17, starting transfers between devices, shift(): return lax.ppermute(a, axis, [(i, (i + by) % size) for i in range(size)])  28.9 us
    pallas_call x13, Pallas kernels, called(): pl.pallas_call(body, out_shape=out_shape, in_specs=list(specs) + [ANY] *...  20.2 us
    ppermute x17, waiting for transfers between devices, shift(): return lax.ppermute(a, axis, [(i, (i + by) % size) for i in range(size)])  19.5 us
    unnamed x64, local copies, waits for them, and re-layouts  18.4 us
    all_to_all x1, waiting for transfers between devices, expert_part(): state = lax.all_to_all(spread, CTX, 0, 0)  9.32 us
    ppermute x1, starting transfers between devices, expert_part(): other = lax.ppermute(mine, 'ep', [(i, i ^ 1) for i in range(experts)])  8.79 us
    ppermute x3, starting transfers between devices, expert_part(): blocks.append(lax.ppermute(total, 'ep', pairs_of))  7.92 us
    all_to_all x1, starting transfers between devices, expert_part(): state = lax.all_to_all(spread, CTX, 0, 0)  6.63 us
  transfers between devices with their start and end apart: 25, of which 11 were waited for; matrix products, arithmetic and copies ran while one was open for 2% of the time, Pallas kernels for 12%

profile of v2, /device:TPU:1, one launch (start us, length us, event | category | flops | bytes accessed | tf_op | source)
XLA Modules:
  0.0 164.0 jit_solution(9680298091186342457)
XLA Ops:
  11.5 2.1 %collective-permute-start = (bf16[8,6144]{1,0:T(8,128)(2,1)}, bf16[8,6144]{1,0:T(8,128)(2,1)S(1)}, u32[]{:S(2)}, u32[]{:S(2)}) collective-permute-start(bf16[8,6144]{1,0:T(8,128)(2,1)} %copy-done.14), channel_id=1, source_target_pairs={{0,8},{8,16},{16,24},{24,0},{1,9},{9,17},{17,25},{25,1},{2,10},{10... | collective-permute-start | bytes 294920 | tf_op jit(solution)/shard_map/ppermute | solution.py:179
  13.6 2.4 %collective-permute-start.1 = (bf16[8,6144]{1,0:T(8,128)(2,1)}, bf16[8,6144]{1,0:T(8,128)(2,1)S(1)}, u32[]{:S(2)}, u32[]{:S(2)}) collective-permute-start(bf16[8,6144]{1,0:T(8,128)(2,1)} %copy-done.14), channel_id=1, source_target_pairs={{0,16},{8,24},{16,0},{24,8},{1,17},{9,25},{17,1},{25,9},{2,18},{10... | collective-permute-start | bytes 294920 | tf_op jit(solution)/shard_map/ppermute | solution.py:179
  24.0 5.7 %collective-permute-start.5 = (bf16[32,6144]{1,0:T(8,128)(2,1)S(1)}, bf16[32,6144]{1,0:T(8,128)(2,1)S(1)}, u32[]{:S(2)}, u32[]{:S(2)}) collective-permute-start(bf16[32,6144]{1,0:T(8,128)(2,1)S(1)} %stack.2.refs_0_), channel_id=1, source_target_pairs={{0,224},{32,0},{64,32},{96,64},{128,96},{160,128},{192,160},{224,1... | collective-permute-start | bytes 1179656 | tf_op jit(solution)/shard_map/ppermute | solution.py:179
  30.4 6.9 %collective-permute-done.5.refs_2_ = bf16[32,6144]{1,0:T(8,128)(2,1)S(1)} collective-permute-done((bf16[32,6144]{1,0:T(8,128)(2,1)S(1)}, bf16[32,6144]{1,0:T(8,128)(2,1)S(1)}, u32[]{:S(2)}, u32[]{:S(2)}) %collective-permute-start.5) | collective-permute-done | bytes 393248 | tf_op jit(solution)/shard_map/ppermute | solution.py:179
  37.2 3.4 %collective-permute-start.6 = (bf16[32,6144]{1,0:T(8,128)(2,1)S(1)}, bf16[32,6144]{1,0:T(8,128)(2,1)}, u32[]{:S(2)}, u32[]{:S(2)}) collective-permute-start(bf16[32,6144]{1,0:T(8,128)(2,1)S(1)} %collective-permute-done.5.refs_2_), channel_id=1, source_target_pairs={{0,224},{32,0},{64,32},{96,64},{128,96},{160,128},{192,160},{224,1... | collective-permute-start | bytes 1179656 | tf_op jit(solution)/shard_map/ppermute | solution.py:179
  42.2 6.5 %collective-permute-done.6.refs_2_.refs_4_ = bf16[32,6144]{1,0:T(8,128)(2,1)} collective-permute-done((bf16[32,6144]{1,0:T(8,128)(2,1)S(1)}, bf16[32,6144]{1,0:T(8,128)(2,1)}, u32[]{:S(2)}, u32[]{:S(2)}) %collective-permute-start.6) | collective-permute-done | bytes 393248 | tf_op jit(solution)/shard_map/ppermute | solution.py:179
  48.6 3.5 %collective-permute-start.8 = (bf16[32,6144]{1,0:T(8,128)(2,1)}, bf16[32,6144]{1,0:T(8,128)(2,1)}, u32[]{:S(2)}, u32[]{:S(2)}) collective-permute-start(bf16[32,6144]{1,0:T(8,128)(2,1)} %collective-permute-done.6.refs_2_.refs_4_), channel_id=1, source_target_pairs={{0,224},{32,0},{64,32},{96,64},{128,96},{160,128},{192,160},{224,1... | collective-permute-start | bytes 1179656 | tf_op jit(solution)/shard_map/ppermute | solution.py:179
  53.1 6.3 %all-to-all-start = ((bf16[32,32,128]{2,1,0:T(8,128)(2,1)}), bf16[32,32,128]{2,1,0:T(8,128)(2,1)}, u32[]{:S(2)}, u32[]{:S(2)}) async-start(bf16[32,32,128]{2,1,0:T(8,128)(2,1)} %copy-done.8), calls=%async_computation | async-start | bytes 524288 | tf_op jit(solution)/shard_map/all_to_all | solution.py:317
  61.0 2.4 %collective-permute-start.10 = (bf16[16,6144]{1,0:T(8,128)(2,1)}, bf16[16,6144]{1,0:T(8,128)(2,1)}, u32[]{:S(2)}, u32[]{:S(2)}) collective-permute-start(bf16[16,6144]{1,0:T(8,128)(2,1)} %slice.9), channel_id=1, source_target_pairs={{0,224},{32,0},{64,32},{96,64},{128,96},{160,128},{192,160},{224,1... | collective-permute-start | bytes 589832 | tf_op jit(solution)/shard_map/ppermute | solution.py:179
  65.1 5.1 %all-to-all-done.refs_0_ = bf16[32,32,128]{2,1,0:T(8,128)(2,1)} async-done(((bf16[32,32,128]{2,1,0:T(8,128)(2,1)}), bf16[32,32,128]{2,1,0:T(8,128)(2,1)}, u32[]{:S(2)}, u32[]{:S(2)}) %all-to-all-start) | async-done | bytes 262176 | tf_op jit(solution)/shard_map/all_to_all | solution.py:317
  73.3 2.1 %copy-done.3 = bf16[1,288,6144]{2,1,0:T(8,128)(2,1)S(1)} copy-done((bf16[1,288,6144]{2,1,0:T(8,128)(2,1)S(1)}, bf16[1,288,6144]{2,1,0:T(8,128)(2,1)}, u32[]{:S(2)}) %copy-start.3) | copy-done | bytes 3538968
  77.6 7.3 %feed_forward.1 = (bf16[64,3072]{1,0:T(8,128)(2,1)S(1)}, bf16[64,3072]{1,0:T(8,128)(2,1)S(1)}, bf16[64,3072]{1,0:T(8,128)(2,1)}, bf16[64,3072]{1,0:T(8,128)(2,1)...) custom-call(bf16[32,6144]{1,0:T(8,128)(2,1)S(1)} %copy-done.5, ...), custom_call_target="tpu_custom_call" | custom-call | flops 2717908992 | bytes 16908288 | tf_op jit(solution)/shard_map/feed_forward/pallas_call | solution.py:36
  87.6 2.7 %collective-permute-start.14 = (bf16[64,3072]{1,0:T(8,128)(2,1)}, bf16[64,3072]{1,0:T(8,128)(2,1)S(1)}, u32[]{:S(2)}, u32[]{:S(2)}) collective-permute-start(bf16[64,3072]{1,0:T(8,128)(2,1)} %get-tuple-element.32), channel_id=1, source_target_pairs={{0,24},{8,0},{16,8},{24,16},{1,25},{9,1},{17,9},{25,17},{2,26},{10... | collective-permute-start | bytes 1179656 | tf_op jit(solution)/shard_map/ppermute | solution.py:179
  90.3 4.1 %collective-permute-done.15.refs_1_ = bf16[64,3072]{1,0:T(8,128)(2,1)S(1)} collective-permute-done((bf16[64,3072]{1,0:T(8,128)(2,1)S(1)}, bf16[64,3072]{1,0:T(8,128)(2,1)S(1)}, u32[]{:S(2)}, u32[]{:S(2)}) %collective-permute-start.15) | collective-permute-done | bytes 393248 | tf_op jit(solution)/shard_map/ppermute | solution.py:179
  94.7 2.7 %collective-permute-start.13 = (bf16[64,3072]{1,0:T(8,128)(2,1)S(1)}, bf16[64,3072]{1,0:T(8,128)(2,1)}, u32[]{:S(2)}, u32[]{:S(2)}) collective-permute-start(bf16[64,3072]{1,0:T(8,128)(2,1)S(1)} %relay.2), channel_id=1, source_target_pairs={{0,24},{8,0},{16,8},{24,16},{1,25},{9,1},{17,9},{25,17},{2,26},{10... | collective-permute-start | bytes 1179656 | tf_op jit(solution)/shard_map/ppermute | solution.py:179
  97.4 6.6 %all-to-all-start.1 = ((bf16[32,16,128]{2,1,0:T(8,128)(2,1)}), bf16[32,16,128]{2,1,0:T(8,128)(2,1)S(1)}, u32[]{:S(2)}, u32[]{:S(2)}) async-start(bf16[32,16,128]{2,1,0:T(8,128)(2,1)} %copy-done.6), calls=%async_computation.1 | async-start | bytes 262144 | tf_op jit(solution)/shard_map/all_to_all | solution.py:341
  104.1 9.3 %all-to-all-done.1.refs_7_.refs_3_ = bf16[32,16,128]{2,1,0:T(8,128)(2,1)S(1)} async-done(((bf16[32,16,128]{2,1,0:T(8,128)(2,1)}), bf16[32,16,128]{2,1,0:T(8,128)(2,1)S(1)}, u32[]{:S(2)}, u32[]{:S(2)}) %all-to-all-start.1) | async-done | bytes 131104 | tf_op jit(solution)/shard_map/all_to_all | solution.py:341
  113.4 2.3 %add_parts.1.refs_4_.refs_3_ = bf16[8,8,6144]{2,1,0:T(8,128)(2,1)} custom-call(s32[1]{0:T(128)} %bitcast.3.refs_0_, bf16[64,3072]{1,0:T(8,128)(2,1)S(1)} %get-tuple-element.27.refs_1_, bf16[64,3072]{1,0:T(8,128)(2,1)S(1)} %collective-permute-done.11.refs_2_, bf16[64,3072]{1,0:T(8,128)(2,1)} %collective-permute-done.13.refs_3_, ...), custom_call_target="tpu_custom_call" | custom-call | tf_op jit(solution)/shard_map/add_parts/pallas_call | solution.py:36
  115.7 4.9 %all-to-all-start.2 = ((bf16[8,8,6144]{2,1,0:T(8,128)(2,1)}), bf16[8,8,6144]{2,1,0:T(8,128)(2,1)S(1)}, u32[]{:S(2)}, u32[]{:S(2)}) async-start(bf16[8,8,6144]{2,1,0:T(8,128)(2,1)} %add_parts.1.refs_4_.refs_3_), calls=%async_computation.2 | async-start | bytes 1572864 | tf_op jit(solution)/shard_map/all_to_all | solution.py:360
  122.9 2.2 %copy-done = bf16[8192,256]{1,0:T(8,128)(2,1)S(1)} copy-done((bf16[8192,256]{1,0:T(8,128)(2,1)S(1)}, bf16[8192,256]{1,0:T(8,128)(2,1)}, u32[]{:S(2)}) %copy-start) | copy-done | bytes 4194328
  125.1 4.3 %sparse_attention.1.refs_1_ = bf16[256,512]{1,0:T(8,128)(2,1)} custom-call(s32[2,8]{1,0:T(2,128)S(1)} %copy-done.29, bf16[256,512]{1,0:T(8,128)(2,1)S(1)} %copy-done.22, bf16[8192,256]{1,0:T(8,128)(2,1)S(1)} %copy-done, bf16[8,8,6144]{2,1,0:T(8,128)(2,1)} %add_parts.1.refs_4_.refs_3_), custom_call_target="tpu_custom_call" | custom-call | tf_op jit(solution)/shard_map/sparse_attention/pallas_call | solution.py:36
  129.4 5.9 %all-to-all-done.2.refs_0_ = bf16[8,8,6144]{2,1,0:T(8,128)(2,1)S(1)} async-done(((bf16[8,8,6144]{2,1,0:T(8,128)(2,1)}), bf16[8,8,6144]{2,1,0:T(8,128)(2,1)S(1)}, u32[]{:S(2)}, u32[]{:S(2)}) %all-to-all-start.2) | async-done | bytes 786464 | tf_op jit(solution)/shard_map/all_to_all | solution.py:360
  137.8 4.5 %collective-permute-start.18 = (bf16[8,6144]{1,0:T(8,128)(2,1)S(1)}, bf16[8,6144]{1,0:T(8,128)(2,1)S(1)}, u32[]{:S(2)}, u32[]{:S(2)}) collective-permute-start(bf16[8,6144]{1,0:T(8,128)(2,1)S(1)} %add_all.1.refs_0_), channel_id=1, source_target_pairs={{0,4},{1,5},{2,6},{3,7},{4,0},{5,1},{6,2},{7,3},{8,12},{9,13},{10,... | collective-permute-start | bytes 294920 | tf_op jit(solution)/shard_map/ppermute | solution.py:373
  145.9 8.8 %collective-permute-start.20 = (bf16[32,6144]{1,0:T(8,128)(2,1)S(1)}, bf16[32,6144]{1,0:T(8,128)(2,1)S(1)}, u32[]{:S(2)}, u32[]{:S(2)}) collective-permute-start(bf16[32,6144]{1,0:T(8,128)(2,1)S(1)} %stack.3.refs_3_), channel_id=1, source_target_pairs={{0,1},{1,0},{2,3},{3,2},{4,5},{5,4},{6,7},{7,6},{8,9},{9,8},{10,11... | collective-permute-start | bytes 1179656 | tf_op jit(solution)/shard_map/ppermute | solution.py:381
  (108 shorter events, 37.7 us)
Async XLA Ops:
  7.2 115.7 %all-gather.2.cloned.1.call-start = ((), (), s32[]{:S(2)}) async-start(), calls=%async_computation.3 | async-start | bytes 4325376 | tf_op jit(solution)/shard_map/all_gather | solution.py:411
  11.5 11.4 %collective-permute-start = (bf16[8,6144]{1,0:T(8,128)(2,1)}, bf16[8,6144]{1,0:T(8,128)(2,1)S(1)}, u32[]{:S(2)}, u32[]{:S(2)}) collective-permute-start(bf16[8,6144]{1,0:T(8,128)(2,1)} %copy-done.14), channel_id=1, source_target_pairs={{0,8},{8,16},{16,24},{24,0},{1,9},{9,17},{17,25},{25,1},{2,10},{10... | collective-permute-start | bytes 294920 | tf_op jit(solution)/shard_map/ppermute | solution.py:179
  13.6 9.3 %collective-permute-start.1 = (bf16[8,6144]{1,0:T(8,128)(2,1)}, bf16[8,6144]{1,0:T(8,128)(2,1)S(1)}, u32[]{:S(2)}, u32[]{:S(2)}) collective-permute-start(bf16[8,6144]{1,0:T(8,128)(2,1)} %copy-done.14), channel_id=1, source_target_pairs={{0,16},{8,24},{16,0},{24,8},{1,17},{9,25},{17,1},{25,9},{2,18},{10... | collective-permute-start | bytes 294920 | tf_op jit(solution)/shard_map/ppermute | solution.py:179
  16.1 6.9 %collective-permute-start.2 = (bf16[8,6144]{1,0:T(8,128)(2,1)}, bf16[8,6144]{1,0:T(8,128)(2,1)S(1)}, u32[]{:S(2)}, u32[]{:S(2)}) collective-permute-start(bf16[8,6144]{1,0:T(8,128)(2,1)} %copy-done.14), channel_id=1, source_target_pairs={{0,24},{8,0},{16,8},{24,16},{1,25},{9,1},{17,9},{25,17},{2,26},{10... | collective-permute-start | bytes 294920 | tf_op jit(solution)/shard_map/ppermute | solution.py:179
  24.0 13.2 %collective-permute-start.5 = (bf16[32,6144]{1,0:T(8,128)(2,1)S(1)}, bf16[32,6144]{1,0:T(8,128)(2,1)S(1)}, u32[]{:S(2)}, u32[]{:S(2)}) collective-permute-start(bf16[32,6144]{1,0:T(8,128)(2,1)S(1)} %stack.2.refs_0_), channel_id=1, source_target_pairs={{0,224},{32,0},{64,32},{96,64},{128,96},{160,128},{192,160},{224,1... | collective-permute-start | bytes 1179656 | tf_op jit(solution)/shard_map/ppermute | solution.py:179
  29.6 11.8 %collective-permute-start.3 = (bf16[32,6144]{1,0:T(8,128)(2,1)S(1)}, bf16[32,6144]{1,0:T(8,128)(2,1)S(1)}, u32[]{:S(2)}, u32[]{:S(2)}) collective-permute-start(bf16[32,6144]{1,0:T(8,128)(2,1)S(1)} %stack.2.refs_0_), channel_id=1, source_target_pairs={{0,32},{32,64},{64,96},{96,128},{128,160},{160,192},{192,224},{224... | collective-permute-start | bytes 1179656 | tf_op jit(solution)/shard_map/ppermute | solution.py:179
  37.2 11.4 %collective-permute-start.6 = (bf16[32,6144]{1,0:T(8,128)(2,1)S(1)}, bf16[32,6144]{1,0:T(8,128)(2,1)}, u32[]{:S(2)}, u32[]{:S(2)}) collective-permute-start(bf16[32,6144]{1,0:T(8,128)(2,1)S(1)} %collective-permute-done.5.refs_2_), channel_id=1, source_target_pairs={{0,224},{32,0},{64,32},{96,64},{128,96},{160,128},{192,160},{224,1... | collective-permute-start | bytes 1179656 | tf_op jit(solution)/shard_map/ppermute | solution.py:179
  41.4 11.7 %collective-permute-start.4 = (bf16[32,6144]{1,0:T(8,128)(2,1)S(1)}, bf16[32,6144]{1,0:T(8,128)(2,1)}, u32[]{:S(2)}, u32[]{:S(2)}) collective-permute-start(bf16[32,6144]{1,0:T(8,128)(2,1)S(1)} %collective-permute-done.3.refs_1_), channel_id=1, source_target_pairs={{0,32},{32,64},{64,96},{96,128},{128,160},{160,192},{192,224},{224... | collective-permute-start | bytes 1179656 | tf_op jit(solution)/shard_map/ppermute | solution.py:179
  48.6 10.8 %collective-permute-start.8 = (bf16[32,6144]{1,0:T(8,128)(2,1)}, bf16[32,6144]{1,0:T(8,128)(2,1)}, u32[]{:S(2)}, u32[]{:S(2)}) collective-permute-start(bf16[32,6144]{1,0:T(8,128)(2,1)} %collective-permute-done.6.refs_2_.refs_4_), channel_id=1, source_target_pairs={{0,224},{32,0},{64,32},{96,64},{128,96},{160,128},{192,160},{224,1... | collective-permute-start | bytes 1179656 | tf_op jit(solution)/shard_map/ppermute | solution.py:179
  53.1 10.4 %collective-permute-start.7 = (bf16[32,6144]{1,0:T(8,128)(2,1)}, bf16[32,6144]{1,0:T(8,128)(2,1)}, u32[]{:S(2)}, u32[]{:S(2)}) collective-permute-start(bf16[32,6144]{1,0:T(8,128)(2,1)} %collective-permute-done.4.refs_1_.refs_3_), channel_id=1, source_target_pairs={{0,32},{32,64},{64,96},{96,128},{128,160},{160,192},{192,224},{224... | collective-permute-start | bytes 1179656 | tf_op jit(solution)/shard_map/ppermute | solution.py:179
  53.1 17.0 %all-to-all-start = ((bf16[32,32,128]{2,1,0:T(8,128)(2,1)}), bf16[32,32,128]{2,1,0:T(8,128)(2,1)}, u32[]{:S(2)}, u32[]{:S(2)}) async-start(bf16[32,32,128]{2,1,0:T(8,128)(2,1)} %copy-done.8), calls=%async_computation | async-start | bytes 524288 | tf_op jit(solution)/shard_map/all_to_all | solution.py:317
  61.0 15.5 %collective-permute-start.10 = (bf16[16,6144]{1,0:T(8,128)(2,1)}, bf16[16,6144]{1,0:T(8,128)(2,1)}, u32[]{:S(2)}, u32[]{:S(2)}) collective-permute-start(bf16[16,6144]{1,0:T(8,128)(2,1)} %slice.9), channel_id=1, source_target_pairs={{0,224},{32,0},{64,32},{96,64},{128,96},{160,128},{192,160},{224,1... | collective-permute-start | bytes 589832 | tf_op jit(solution)/shard_map/ppermute | solution.py:179
  65.1 12.5 %collective-permute-start.9 = (bf16[16,6144]{1,0:T(8,128)(2,1)}, bf16[16,6144]{1,0:T(8,128)(2,1)}, u32[]{:S(2)}, u32[]{:S(2)}) collective-permute-start(bf16[16,6144]{1,0:T(8,128)(2,1)} %slice.8), channel_id=1, source_target_pairs={{0,32},{32,64},{64,96},{96,128},{128,160},{160,192},{192,224},{224... | collective-permute-start | bytes 589832 | tf_op jit(solution)/shard_map/ppermute | solution.py:179
  84.9 9.5 %collective-permute-start.15 = (bf16[64,3072]{1,0:T(8,128)(2,1)S(1)}, bf16[64,3072]{1,0:T(8,128)(2,1)S(1)}, u32[]{:S(2)}, u32[]{:S(2)}) collective-permute-start(bf16[64,3072]{1,0:T(8,128)(2,1)S(1)} %get-tuple-element.34), channel_id=1, source_target_pairs={{0,8},{8,16},{16,24},{24,0},{1,9},{9,17},{17,25},{25,1},{2,10},{10... | collective-permute-start | bytes 1179656 | tf_op jit(solution)/shard_map/ppermute | solution.py:179
  85.7 8.9 %collective-permute-start.12 = (bf16[64,3072]{1,0:T(8,128)(2,1)S(1)}, bf16[64,3072]{1,0:T(8,128)(2,1)S(1)}, u32[]{:S(2)}, u32[]{:S(2)}) collective-permute-start(bf16[64,3072]{1,0:T(8,128)(2,1)S(1)} %get-tuple-element.30), channel_id=1, source_target_pairs={{0,24},{8,0},{16,8},{24,16},{1,25},{9,1},{17,9},{25,17},{2,26},{10... | collective-permute-start | bytes 1179656 | tf_op jit(solution)/shard_map/ppermute | solution.py:179
  87.6 25.8 %collective-permute-start.11 = (bf16[64,3072]{1,0:T(8,128)(2,1)}, bf16[64,3072]{1,0:T(8,128)(2,1)S(1)}, u32[]{:S(2)}, u32[]{:S(2)}) collective-permute-start(bf16[64,3072]{1,0:T(8,128)(2,1)} %get-tuple-element.28), channel_id=1, source_target_pairs={{0,8},{8,16},{16,24},{24,0},{1,9},{9,17},{17,25},{25,1},{2,10},{10... | collective-permute-start | bytes 1179656 | tf_op jit(solution)/shard_map/ppermute | solution.py:179
  87.6 25.8 %collective-permute-start.14 = (bf16[64,3072]{1,0:T(8,128)(2,1)}, bf16[64,3072]{1,0:T(8,128)(2,1)S(1)}, u32[]{:S(2)}, u32[]{:S(2)}) collective-permute-start(bf16[64,3072]{1,0:T(8,128)(2,1)} %get-tuple-element.32), channel_id=1, source_target_pairs={{0,24},{8,0},{16,8},{24,16},{1,25},{9,1},{17,9},{25,17},{2,26},{10... | collective-permute-start | bytes 1179656 | tf_op jit(solution)/shard_map/ppermute | solution.py:179
  94.5 18.9 %collective-permute-start.16 = (bf16[64,3072]{1,0:T(8,128)(2,1)S(1)}, bf16[64,3072]{1,0:T(8,128)(2,1)}, u32[]{:S(2)}, u32[]{:S(2)}) collective-permute-start(bf16[64,3072]{1,0:T(8,128)(2,1)S(1)} %relay.3), channel_id=1, source_target_pairs={{0,8},{8,16},{16,24},{24,0},{1,9},{9,17},{17,25},{25,1},{2,10},{10... | collective-permute-start | bytes 1179656 | tf_op jit(solution)/shard_map/ppermute | solution.py:179
  94.7 18.7 %collective-permute-start.13 = (bf16[64,3072]{1,0:T(8,128)(2,1)S(1)}, bf16[64,3072]{1,0:T(8,128)(2,1)}, u32[]{:S(2)}, u32[]{:S(2)}) collective-permute-start(bf16[64,3072]{1,0:T(8,128)(2,1)S(1)} %relay.2), channel_id=1, source_target_pairs={{0,24},{8,0},{16,8},{24,16},{1,25},{9,1},{17,9},{25,17},{2,26},{10... | collective-permute-start | bytes 1179656 | tf_op jit(solution)/shard_map/ppermute | solution.py:179
  97.4 16.0 %all-to-all-start.1 = ((bf16[32,16,128]{2,1,0:T(8,128)(2,1)}), bf16[32,16,128]{2,1,0:T(8,128)(2,1)S(1)}, u32[]{:S(2)}, u32[]{:S(2)}) async-start(bf16[32,16,128]{2,1,0:T(8,128)(2,1)} %copy-done.6), calls=%async_computation.1 | async-start | bytes 262144 | tf_op jit(solution)/shard_map/all_to_all | solution.py:341
  115.7 19.5 %all-to-all-start.2 = ((bf16[8,8,6144]{2,1,0:T(8,128)(2,1)}), bf16[8,8,6144]{2,1,0:T(8,128)(2,1)S(1)}, u32[]{:S(2)}, u32[]{:S(2)}) async-start(bf16[8,8,6144]{2,1,0:T(8,128)(2,1)} %add_parts.1.refs_4_.refs_3_), calls=%async_computation.2 | async-start | bytes 1572864 | tf_op jit(solution)/shard_map/all_to_all | solution.py:360
  136.3 7.9 %collective-permute-start.17 = (bf16[8,6144]{1,0:T(8,128)(2,1)S(1)}, bf16[8,6144]{1,0:T(8,128)(2,1)S(1)}, u32[]{:S(2)}, u32[]{:S(2)}) collective-permute-start(bf16[8,6144]{1,0:T(8,128)(2,1)S(1)} %add_all.1.refs_0_), channel_id=1, source_target_pairs={{0,2},{1,3},{2,4},{3,5},{4,6},{5,7},{6,0},{7,1},{8,10},{9,11},{10,... | collective-permute-start | bytes 294920 | tf_op jit(solution)/shard_map/ppermute | solution.py:373
  137.8 7.4 %collective-permute-start.18 = (bf16[8,6144]{1,0:T(8,128)(2,1)S(1)}, bf16[8,6144]{1,0:T(8,128)(2,1)S(1)}, u32[]{:S(2)}, u32[]{:S(2)}) collective-permute-start(bf16[8,6144]{1,0:T(8,128)(2,1)S(1)} %add_all.1.refs_0_), channel_id=1, source_target_pairs={{0,4},{1,5},{2,6},{3,7},{4,0},{5,1},{6,2},{7,3},{8,12},{9,13},{10,... | collective-permute-start | bytes 294920 | tf_op jit(solution)/shard_map/ppermute | solution.py:373
  145.9 10.1 %collective-permute-start.20 = (bf16[32,6144]{1,0:T(8,128)(2,1)S(1)}, bf16[32,6144]{1,0:T(8,128)(2,1)S(1)}, u32[]{:S(2)}, u32[]{:S(2)}) collective-permute-start(bf16[32,6144]{1,0:T(8,128)(2,1)S(1)} %stack.3.refs_3_), channel_id=1, source_target_pairs={{0,1},{1,0},{2,3},{3,2},{4,5},{5,4},{6,7},{7,6},{8,9},{9,8},{10,11... | collective-permute-start | bytes 1179656 | tf_op jit(solution)/shard_map/ppermute | solution.py:381
  (32 other events, 319.2 us)
Sparse Core Ops, SparseCore 0:
  11.6 84.5 all-gather.1

commit v3 on v2

--- a/solution.py
+++ b/solution.py
@@ -214,6 +214,12 @@
             ref[:, at : at + width] = parts[k]
 
 
+def cut(ahead_ref, back_ref, first_ref, second_ref):
+    half = first_ref.shape[0]
+    first_ref[...] = ahead_ref[:half]
+    second_ref[...] = back_ref[half:]
+
+
 def load(*refs):
     sems = refs[-1]
     copies = [pltpu.make_async_copy(refs[n], refs[n + 3], sems.at[n]) for n in range(3)]
@@ -316,10 +322,13 @@
     ahead1, back1 = shift(own, "z", 1), shift(own, "z", -1)
     got = lax.all_to_all(send, CTX, 0, 0)
     ahead2, back2 = shift(ahead1, "z", 1), shift(back1, "z", -1)
-    spread = states(got, (ahead2, back2))
+    spread = states(got, (ahead1, back1))
+    state = lax.all_to_all(spread, CTX, 0, 0)
     ahead3, back3 = shift(ahead2, "z", 1), shift(back2, "z", -1)
-    weights = loaded(weights, (ahead3, back3))
-    far = [shift(ahead3[:half], "z", 1), shift(back3[half:], "z", -1)]
+    weights = loaded(weights, (ahead3, back3, state))
+    halves = (jax.ShapeDtypeStruct((half, width), BF16),) * 2
+    first, second = called(cut, halves, (ahead3, back3), [VMEM] * 2, (), name="cut")
+    far = [shift(first, "z", 1), shift(second, "z", -1)]
     blocks = [own, ahead1, back1, ahead2, back2, ahead3, back3] + far
     rows = sum(block.shape[0] for block in blocks)
     part = jax.ShapeDtypeStruct((rows // X, width // 2), BF16)
@@ -328,7 +337,7 @@
         (part,) * 8,
         (*blocks, *weights),
         [VMEM] * (len(blocks) + 3),
-        (spread,),
+        (state,),
         (),
         24,
         pl.CostEstimate(
@@ -338,7 +347,6 @@
         ),
         "feed_forward",
     )
-    state = lax.all_to_all(spread, CTX, 0, 0)
     parts = []
     for side in range(2):
         here, minus, plus, mine = leaving[4 * side : 4 * side + 4]
@@ -352,7 +360,6 @@
         jax.ShapeDtypeStruct((many, CAP, width), BF16),
         (lax.axis_index("z").astype(jnp.int32).reshape(1), *parts),
         [SMEM] + [VMEM] * 6,
-        (state,),
         name="add_parts",
     )
     lin_mixed = finish(inside, cumul, state, (sums,))

time: 165 us -> 163 us (0.988)
  waiting for transfers between devices: 42.6 us -> 48.2 us
  local copies, waits for them, and re-layouts: 21.6 us -> 17.5 us
  starting transfers between devices: 63.5 us -> 59.5 us
    ppermute x17, waiting for transfers between devices: 19.5 us -> 26.2 us  [shift(): return lax.ppermute(a, axis, [(i, (i + by) % size) for i in range(size)])]
    all_to_all x1, waiting for transfers between devices: 9.32 us -> 5.34 us  [expert_part(): state = lax.all_to_all(spread, CTX, 0, 0)]
    ppermute x3, starting transfers between devices: 7.92 us -> 4.43 us  [expert_part(): blocks.append(lax.ppermute(total, 'ep', pairs_of))]
    slice x2 -> x0, local copies, waits for them, and re-layouts: 3.23 us -> none  [expert_part(): far = [shift(ahead3[:half], 'z', 1), shift(back3[half:], 'z', -1)]]
    ppermute x1, starting transfers between devices: 8.79 us -> 11.6 us  [expert_part(): other = lax.ppermute(mine, 'ep', [(i, i ^ 1) for i in range(experts)])]
    ppermute x3, waiting for transfers between devices: 1.64 us -> 3.65 us  [expert_part(): blocks.append(lax.ppermute(total, 'ep', pairs_of))]
    unnamed x64 -> x48, local copies, waits for them, and re-layouts: 18.4 us -> 17.5 us
    pallas_call x13 -> x14, Pallas kernels: 20.2 us -> 20.8 us  [called(): pl.pallas_call(body, out_shape=out_shape, in_specs=list(specs) + [ANY] *...]
  transfers between devices with their start and end apart: 25 -> 25, of which waited for: 11 -> 14; matrix products, arithmetic and copies ran while one was open for 2% -> 0% of each run, Pallas kernels for 12% -> 12%
where the time goes in v3:
time: 163 us; the launch traced here: 162 us
  starting transfers between devices  59.5 us (37%)
  waiting for transfers between devices  48.2 us (30%)
  Pallas kernels  21.1 us (13%)
  local copies, waits for them, and re-layouts  17.5 us (11%)
  between operations  14.2 us (9%)
    ppermute x17, starting transfers between devices, shift(): return lax.ppermute(a, axis, [(i, (i + by) % size) for i in range(size)])  27.4 us
    ppermute x17, waiting for transfers between devices, shift(): return lax.ppermute(a, axis, [(i, (i + by) % size) for i in range(size)])  26.2 us
    pallas_call x14, Pallas kernels, called(): pl.pallas_call(body, out_shape=out_shape, in_specs=list(specs) + [ANY] *...  20.8 us
    unnamed x48, local copies, waits for them, and re-layouts  17.5 us
    ppermute x1, starting transfers between devices, expert_part(): other = lax.ppermute(mine, 'ep', [(i, i ^ 1) for i in range(experts)])  11.6 us
    all_to_all x1, waiting for transfers between devices, expert_part(): sums = lax.all_to_all(sums, 'z', 0, 0)  6.32 us
    all_to_all x1, starting transfers between devices, expert_part(): got = lax.all_to_all(send, CTX, 0, 0)  6.23 us
    all_to_all x1, starting transfers between devices, expert_part(): state = lax.all_to_all(spread, CTX, 0, 0)  5.81 us
  transfers between devices with their start and end apart: 25, of which 14 were waited for; matrix products, arithmetic and copies ran while one was open for 0% of the time, Pallas kernels for 12%

profile of v3, /device:TPU:1, one launch (start us, length us, event | category | flops | bytes accessed | tf_op | source)
XLA Modules:
  0.0 162.1 jit_solution(14053926605773805365)
XLA Ops:
  12.8 2.5 %collective-permute-start.1 = (bf16[8,6144]{1,0:T(8,128)(2,1)S(1)}, bf16[8,6144]{1,0:T(8,128)(2,1)S(1)}, u32[]{:S(2)}, u32[]{:S(2)}) collective-permute-start(bf16[8,6144]{1,0:T(8,128)(2,1)S(1)} %pick_tokens.1.refs_0_), channel_id=1, source_target_pairs={{0,16},{8,24},{16,0},{24,8},{1,17},{9,25},{17,1},{25,9},{2,18},{10... | collective-permute-start | bytes 294920 | tf_op jit(solution)/shard_map/ppermute | solution.py:179
  23.8 4.0 %collective-permute-start.4 = (bf16[32,6144]{1,0:T(8,128)(2,1)S(1)}, bf16[32,6144]{1,0:T(8,128)(2,1)S(1)}, u32[]{:S(2)}, u32[]{:S(2)}) collective-permute-start(bf16[32,6144]{1,0:T(8,128)(2,1)S(1)} %stack.2.refs_0_), channel_id=1, source_target_pairs={{0,224},{32,0},{64,32},{96,64},{128,96},{160,128},{192,160},{224,1... | collective-permute-start | bytes 1179656 | tf_op jit(solution)/shard_map/ppermute | solution.py:179
  27.8 8.7 %collective-permute-done.3.refs_1_ = bf16[32,6144]{1,0:T(8,128)(2,1)S(1)} collective-permute-done((bf16[32,6144]{1,0:T(8,128)(2,1)S(1)}, bf16[32,6144]{1,0:T(8,128)(2,1)S(1)}, u32[]{:S(2)}, u32[]{:S(2)}) %collective-permute-start.3) | collective-permute-done | bytes 393248 | tf_op jit(solution)/shard_map/ppermute | solution.py:179
  36.5 3.0 %collective-permute-start.6 = (bf16[32,6144]{1,0:T(8,128)(2,1)S(1)}, bf16[32,6144]{1,0:T(8,128)(2,1)}, u32[]{:S(2)}, u32[]{:S(2)}) collective-permute-start(bf16[32,6144]{1,0:T(8,128)(2,1)S(1)} %collective-permute-done.4.refs_2_), channel_id=1, source_target_pairs={{0,224},{32,0},{64,32},{96,64},{128,96},{160,128},{192,160},{224,1... | collective-permute-start | bytes 1179656 | tf_op jit(solution)/shard_map/ppermute | solution.py:179
  39.5 6.2 %all-to-all-start = ((bf16[32,32,128]{2,1,0:T(8,128)(2,1)}), bf16[32,32,128]{2,1,0:T(8,128)(2,1)S(1)}, u32[]{:S(2)}, u32[]{:S(2)}) async-start(bf16[32,32,128]{2,1,0:T(8,128)(2,1)} %get-tuple-element.24.refs_4_), calls=%async_computation | async-start | bytes 524288 | tf_op jit(solution)/shard_map/all_to_all | solution.py:323
  47.9 3.2 %collective-permute-start.8 = (bf16[32,6144]{1,0:T(8,128)(2,1)}, bf16[32,6144]{1,0:T(8,128)(2,1)S(1)}, u32[]{:S(2)}, u32[]{:S(2)}) collective-permute-start(bf16[32,6144]{1,0:T(8,128)(2,1)} %collective-permute-done.6.refs_4_), channel_id=1, source_target_pairs={{0,224},{32,0},{64,32},{96,64},{128,96},{160,128},{192,160},{224,1... | collective-permute-start | bytes 1179656 | tf_op jit(solution)/shard_map/ppermute | solution.py:179
  51.1 5.5 %all-to-all-done.refs_0_ = bf16[32,32,128]{2,1,0:T(8,128)(2,1)S(1)} async-done(((bf16[32,32,128]{2,1,0:T(8,128)(2,1)}), bf16[32,32,128]{2,1,0:T(8,128)(2,1)S(1)}, u32[]{:S(2)}, u32[]{:S(2)}) %all-to-all-start) | async-done | bytes 262176 | tf_op jit(solution)/shard_map/all_to_all | solution.py:323
  57.3 5.8 %all-to-all-start.1 = ((bf16[32,16,128]{2,1,0:T(8,128)(2,1)}), bf16[32,16,128]{2,1,0:T(8,128)(2,1)S(1)}, u32[]{:S(2)}, u32[]{:S(2)}) async-start(bf16[32,16,128]{2,1,0:T(8,128)(2,1)} %lightning_chain.1), calls=%async_computation.1 | async-start | bytes 262144 | tf_op jit(solution)/shard_map/all_to_all | solution.py:326
  67.1 5.3 %all-to-all-done.1.refs_5_.refs_12_.refs_3_ = bf16[32,16,128]{2,1,0:T(8,128)(2,1)S(1)} async-done(((bf16[32,16,128]{2,1,0:T(8,128)(2,1)}), bf16[32,16,128]{2,1,0:T(8,128)(2,1)S(1)}, u32[]{:S(2)}, u32[]{:S(2)}) %all-to-all-start.1) | async-done | bytes 131104 | tf_op jit(solution)/shard_map/all_to_all | solution.py:326
  80.9 6.8 %feed_forward.1 = (bf16[64,3072]{1,0:T(8,128)(2,1)S(1)}, bf16[64,3072]{1,0:T(8,128)(2,1)S(1)}, bf16[64,3072]{1,0:T(8,128)(2,1)}, bf16[64,3072]{1,0:T(8,128)(2,1)...) custom-call(bf16[32,6144]{1,0:T(8,128)(2,1)S(1)} %stack.2.refs_0_, ...), custom_call_target="tpu_custom_call" | custom-call | flops 2717908992 | bytes 16908288 | tf_op jit(solution)/shard_map/feed_forward/pallas_call | solution.py:36
  89.2 2.6 %collective-permute-start.14 = (bf16[64,3072]{1,0:T(8,128)(2,1)}, bf16[64,3072]{1,0:T(8,128)(2,1)S(1)}, u32[]{:S(2)}, u32[]{:S(2)}) collective-permute-start(bf16[64,3072]{1,0:T(8,128)(2,1)} %get-tuple-element.36), channel_id=1, source_target_pairs={{0,24},{8,0},{16,8},{24,16},{1,25},{9,1},{17,9},{25,17},{2,26},{10... | collective-permute-start | bytes 1179656 | tf_op jit(solution)/shard_map/ppermute | solution.py:179
  91.8 2.7 %collective-permute-done.12.refs_1_ = bf16[64,3072]{1,0:T(8,128)(2,1)S(1)} collective-permute-done((bf16[64,3072]{1,0:T(8,128)(2,1)S(1)}, bf16[64,3072]{1,0:T(8,128)(2,1)S(1)}, u32[]{:S(2)}, u32[]{:S(2)}) %collective-permute-start.12) | collective-permute-done | bytes 393248 | tf_op jit(solution)/shard_map/ppermute | solution.py:179
  94.6 2.8 %collective-permute-start.13 = (bf16[64,3072]{1,0:T(8,128)(2,1)S(1)}, bf16[64,3072]{1,0:T(8,128)(2,1)S(1)}, u32[]{:S(2)}, u32[]{:S(2)}) collective-permute-start(bf16[64,3072]{1,0:T(8,128)(2,1)S(1)} %relay.2), channel_id=1, source_target_pairs={{0,24},{8,0},{16,8},{24,16},{1,25},{9,1},{17,9},{25,17},{2,26},{10... | collective-permute-start | bytes 1179656 | tf_op jit(solution)/shard_map/ppermute | solution.py:179
  97.6 3.4 %collective-permute-done.11.refs_2_ = bf16[64,3072]{1,0:T(8,128)(2,1)S(1)} collective-permute-done((bf16[64,3072]{1,0:T(8,128)(2,1)}, bf16[64,3072]{1,0:T(8,128)(2,1)S(1)}, u32[]{:S(2)}, u32[]{:S(2)}) %collective-permute-start.11) | collective-permute-done | bytes 393248 | tf_op jit(solution)/shard_map/ppermute | solution.py:179
  101.0 5.7 %collective-permute-done.13.refs_3_ = bf16[64,3072]{1,0:T(8,128)(2,1)S(1)} collective-permute-done((bf16[64,3072]{1,0:T(8,128)(2,1)S(1)}, bf16[64,3072]{1,0:T(8,128)(2,1)S(1)}, u32[]{:S(2)}, u32[]{:S(2)}) %collective-permute-start.13) | collective-permute-done | bytes 393248 | tf_op jit(solution)/shard_map/ppermute | solution.py:179
  106.8 2.9 %collective-permute-done.16.refs_6_ = bf16[64,3072]{1,0:T(8,128)(2,1)} collective-permute-done((bf16[64,3072]{1,0:T(8,128)(2,1)S(1)}, bf16[64,3072]{1,0:T(8,128)(2,1)}, u32[]{:S(2)}, u32[]{:S(2)}) %collective-permute-start.16) | collective-permute-done | bytes 393248 | tf_op jit(solution)/shard_map/ppermute | solution.py:179
  110.7 2.2 %add_parts.1.refs_4_.refs_3_ = bf16[8,8,6144]{2,1,0:T(8,128)(2,1)} custom-call(s32[1]{0:T(128)} %bitcast.3.refs_0_, bf16[64,3072]{1,0:T(8,128)(2,1)S(1)} %get-tuple-element.31.refs_1_, bf16[64,3072]{1,0:T(8,128)(2,1)S(1)} %collective-permute-done.11.refs_2_, bf16[64,3072]{1,0:T(8,128)(2,1)S(1)} %collective-permute-done.13.refs_3_, ...), custom_call_target="tpu_custom_call" | custom-call | tf_op jit(solution)/shard_map/add_parts/pallas_call | solution.py:36
  112.9 4.1 %all-to-all-start.2 = ((bf16[8,8,6144]{2,1,0:T(8,128)(2,1)}), bf16[8,8,6144]{2,1,0:T(8,128)(2,1)S(1)}, u32[]{:S(2)}, u32[]{:S(2)}) async-start(bf16[8,8,6144]{2,1,0:T(8,128)(2,1)} %add_parts.1.refs_4_.refs_3_), calls=%async_computation.2 | async-start | bytes 1572864 | tf_op jit(solution)/shard_map/all_to_all | solution.py:367
  119.2 2.2 %copy-done = bf16[8192,256]{1,0:T(8,128)(2,1)S(1)} copy-done((bf16[8192,256]{1,0:T(8,128)(2,1)S(1)}, bf16[8192,256]{1,0:T(8,128)(2,1)}, u32[]{:S(2)}) %copy-start) | copy-done | bytes 4194328
  121.3 4.3 %sparse_attention.1.refs_1_ = bf16[256,512]{1,0:T(8,128)(2,1)} custom-call(s32[2,8]{1,0:T(2,128)S(1)} %copy-done.21, bf16[256,512]{1,0:T(8,128)(2,1)S(1)} %copy-done.14, bf16[8192,256]{1,0:T(8,128)(2,1)S(1)} %copy-done, bf16[8,8,6144]{2,1,0:T(8,128)(2,1)} %add_parts.1.refs_4_.refs_3_), custom_call_target="tpu_custom_call" | custom-call | tf_op jit(solution)/shard_map/sparse_attention/pallas_call | solution.py:36
  125.7 6.3 %all-to-all-done.2.refs_0_ = bf16[8,8,6144]{2,1,0:T(8,128)(2,1)S(1)} async-done(((bf16[8,8,6144]{2,1,0:T(8,128)(2,1)}), bf16[8,8,6144]{2,1,0:T(8,128)(2,1)S(1)}, u32[]{:S(2)}, u32[]{:S(2)}) %all-to-all-start.2) | async-done | bytes 786464 | tf_op jit(solution)/shard_map/all_to_all | solution.py:367
  133.9 3.4 %collective-permute-start.18 = (bf16[8,6144]{1,0:T(8,128)(2,1)S(1)}, bf16[8,6144]{1,0:T(8,128)(2,1)S(1)}, u32[]{:S(2)}, u32[]{:S(2)}) collective-permute-start(bf16[8,6144]{1,0:T(8,128)(2,1)S(1)} %add_all.1.refs_0_), channel_id=1, source_target_pairs={{0,4},{1,5},{2,6},{3,7},{4,0},{5,1},{6,2},{7,3},{8,12},{9,13},{10,... | collective-permute-start | bytes 294920 | tf_op jit(solution)/shard_map/ppermute | solution.py:380
  138.2 2.5 %collective-permute-done.18.refs_2_ = bf16[8,6144]{1,0:T(8,128)(2,1)S(1)} collective-permute-done((bf16[8,6144]{1,0:T(8,128)(2,1)S(1)}, bf16[8,6144]{1,0:T(8,128)(2,1)S(1)}, u32[]{:S(2)}, u32[]{:S(2)}) %collective-permute-start.18) | collective-permute-done | bytes 98336 | tf_op jit(solution)/shard_map/ppermute | solution.py:380
  141.2 11.6 %collective-permute-start.20 = (bf16[32,6144]{1,0:T(8,128)(2,1)S(1)}, bf16[32,6144]{1,0:T(8,128)(2,1)S(1)}, u32[]{:S(2)}, u32[]{:S(2)}) collective-permute-start(bf16[32,6144]{1,0:T(8,128)(2,1)S(1)} %stack.3.refs_3_), channel_id=1, source_target_pairs={{0,1},{1,0},{2,3},{3,2},{4,5},{5,4},{6,7},{7,6},{8,9},{9,8},{10,11... | collective-permute-start | bytes 1179656 | tf_op jit(solution)/shard_map/ppermute | solution.py:388
  (91 shorter events, 39.9 us)
Async XLA Ops:
  7.2 112.0 %all-gather.2.cloned.1.call-start = ((), (), s32[]{:S(2)}) async-start(), calls=%async_computation.3 | async-start | bytes 4325376 | tf_op jit(solution)/shard_map/all_gather | solution.py:418
  10.7 11.3 %collective-permute-start = (bf16[8,6144]{1,0:T(8,128)(2,1)S(1)}, bf16[8,6144]{1,0:T(8,128)(2,1)S(1)}, u32[]{:S(2)}, u32[]{:S(2)}) collective-permute-start(bf16[8,6144]{1,0:T(8,128)(2,1)S(1)} %pick_tokens.1.refs_0_), channel_id=1, source_target_pairs={{0,8},{8,16},{16,24},{24,0},{1,9},{9,17},{17,25},{25,1},{2,10},{10... | collective-permute-start | bytes 294920 | tf_op jit(solution)/shard_map/ppermute | solution.py:179
  12.8 9.2 %collective-permute-start.1 = (bf16[8,6144]{1,0:T(8,128)(2,1)S(1)}, bf16[8,6144]{1,0:T(8,128)(2,1)S(1)}, u32[]{:S(2)}, u32[]{:S(2)}) collective-permute-start(bf16[8,6144]{1,0:T(8,128)(2,1)S(1)} %pick_tokens.1.refs_0_), channel_id=1, source_target_pairs={{0,16},{8,24},{16,0},{24,8},{1,17},{9,25},{17,1},{25,9},{2,18},{10... | collective-permute-start | bytes 294920 | tf_op jit(solution)/shard_map/ppermute | solution.py:179
  15.3 6.7 %collective-permute-start.2 = (bf16[8,6144]{1,0:T(8,128)(2,1)S(1)}, bf16[8,6144]{1,0:T(8,128)(2,1)S(1)}, u32[]{:S(2)}, u32[]{:S(2)}) collective-permute-start(bf16[8,6144]{1,0:T(8,128)(2,1)S(1)} %pick_tokens.1.refs_0_), channel_id=1, source_target_pairs={{0,24},{8,0},{16,8},{24,16},{1,25},{9,1},{17,9},{25,17},{2,26},{10... | collective-permute-start | bytes 294920 | tf_op jit(solution)/shard_map/ppermute | solution.py:179
  22.0 14.5 %collective-permute-start.3 = (bf16[32,6144]{1,0:T(8,128)(2,1)S(1)}, bf16[32,6144]{1,0:T(8,128)(2,1)S(1)}, u32[]{:S(2)}, u32[]{:S(2)}) collective-permute-start(bf16[32,6144]{1,0:T(8,128)(2,1)S(1)} %stack.2.refs_0_), channel_id=1, source_target_pairs={{0,32},{32,64},{64,96},{96,128},{128,160},{160,192},{192,224},{224... | collective-permute-start | bytes 1179656 | tf_op jit(solution)/shard_map/ppermute | solution.py:179
  23.8 12.7 %collective-permute-start.4 = (bf16[32,6144]{1,0:T(8,128)(2,1)S(1)}, bf16[32,6144]{1,0:T(8,128)(2,1)S(1)}, u32[]{:S(2)}, u32[]{:S(2)}) collective-permute-start(bf16[32,6144]{1,0:T(8,128)(2,1)S(1)} %stack.2.refs_0_), channel_id=1, source_target_pairs={{0,224},{32,0},{64,32},{96,64},{128,96},{160,128},{192,160},{224,1... | collective-permute-start | bytes 1179656 | tf_op jit(solution)/shard_map/ppermute | solution.py:179
  36.5 11.4 %collective-permute-start.5 = (bf16[32,6144]{1,0:T(8,128)(2,1)S(1)}, bf16[32,6144]{1,0:T(8,128)(2,1)S(1)}, u32[]{:S(2)}, u32[]{:S(2)}) collective-permute-start(bf16[32,6144]{1,0:T(8,128)(2,1)S(1)} %collective-permute-done.3.refs_1_), channel_id=1, source_target_pairs={{0,32},{32,64},{64,96},{96,128},{128,160},{160,192},{192,224},{224... | collective-permute-start | bytes 1179656 | tf_op jit(solution)/shard_map/ppermute | solution.py:179
  36.5 11.4 %collective-permute-start.6 = (bf16[32,6144]{1,0:T(8,128)(2,1)S(1)}, bf16[32,6144]{1,0:T(8,128)(2,1)}, u32[]{:S(2)}, u32[]{:S(2)}) collective-permute-start(bf16[32,6144]{1,0:T(8,128)(2,1)S(1)} %collective-permute-done.4.refs_2_), channel_id=1, source_target_pairs={{0,224},{32,0},{64,32},{96,64},{128,96},{160,128},{192,160},{224,1... | collective-permute-start | bytes 1179656 | tf_op jit(solution)/shard_map/ppermute | solution.py:179
  39.5 17.0 %all-to-all-start = ((bf16[32,32,128]{2,1,0:T(8,128)(2,1)}), bf16[32,32,128]{2,1,0:T(8,128)(2,1)S(1)}, u32[]{:S(2)}, u32[]{:S(2)}) async-start(bf16[32,32,128]{2,1,0:T(8,128)(2,1)} %get-tuple-element.24.refs_4_), calls=%async_computation | async-start | bytes 524288 | tf_op jit(solution)/shard_map/all_to_all | solution.py:323
  47.9 15.8 %collective-permute-start.7 = (bf16[32,6144]{1,0:T(8,128)(2,1)S(1)}, bf16[32,6144]{1,0:T(8,128)(2,1)S(1)}, u32[]{:S(2)}, u32[]{:S(2)}) collective-permute-start(bf16[32,6144]{1,0:T(8,128)(2,1)S(1)} %collective-permute-done.5.refs_3_), channel_id=1, source_target_pairs={{0,32},{32,64},{64,96},{96,128},{128,160},{160,192},{192,224},{224... | collective-permute-start | bytes 1179656 | tf_op jit(solution)/shard_map/ppermute | solution.py:179
  47.9 15.8 %collective-permute-start.8 = (bf16[32,6144]{1,0:T(8,128)(2,1)}, bf16[32,6144]{1,0:T(8,128)(2,1)S(1)}, u32[]{:S(2)}, u32[]{:S(2)}) collective-permute-start(bf16[32,6144]{1,0:T(8,128)(2,1)} %collective-permute-done.6.refs_4_), channel_id=1, source_target_pairs={{0,224},{32,0},{64,32},{96,64},{128,96},{160,128},{192,160},{224,1... | collective-permute-start | bytes 1179656 | tf_op jit(solution)/shard_map/ppermute | solution.py:179
  57.3 15.2 %all-to-all-start.1 = ((bf16[32,16,128]{2,1,0:T(8,128)(2,1)}), bf16[32,16,128]{2,1,0:T(8,128)(2,1)S(1)}, u32[]{:S(2)}, u32[]{:S(2)}) async-start(bf16[32,16,128]{2,1,0:T(8,128)(2,1)} %lightning_chain.1), calls=%async_computation.1 | async-start | bytes 262144 | tf_op jit(solution)/shard_map/all_to_all | solution.py:326
  64.4 15.4 %collective-permute-start.9 = (bf16[16,6144]{1,0:T(8,128)(2,1)}, bf16[16,6144]{1,0:T(8,128)(2,1)S(1)}, u32[]{:S(2)}, u32[]{:S(2)}) collective-permute-start(bf16[16,6144]{1,0:T(8,128)(2,1)} %get-tuple-element.26), channel_id=1, source_target_pairs={{0,32},{32,64},{64,96},{96,128},{128,160},{160,192},{192,224},{224... | collective-permute-start | bytes 589832 | tf_op jit(solution)/shard_map/ppermute | solution.py:179
  65.1 14.7 %collective-permute-start.10 = (bf16[16,6144]{1,0:T(8,128)(2,1)}, bf16[16,6144]{1,0:T(8,128)(2,1)S(1)}, u32[]{:S(2)}, u32[]{:S(2)}) collective-permute-start(bf16[16,6144]{1,0:T(8,128)(2,1)} %get-tuple-element.27), channel_id=1, source_target_pairs={{0,224},{32,0},{64,32},{96,64},{128,96},{160,128},{192,160},{224,1... | collective-permute-start | bytes 589832 | tf_op jit(solution)/shard_map/ppermute | solution.py:179
  87.7 6.8 %collective-permute-start.12 = (bf16[64,3072]{1,0:T(8,128)(2,1)S(1)}, bf16[64,3072]{1,0:T(8,128)(2,1)S(1)}, u32[]{:S(2)}, u32[]{:S(2)}) collective-permute-start(bf16[64,3072]{1,0:T(8,128)(2,1)S(1)} %get-tuple-element.34), channel_id=1, source_target_pairs={{0,24},{8,0},{16,8},{24,16},{1,25},{9,1},{17,9},{25,17},{2,26},{10... | collective-permute-start | bytes 1179656 | tf_op jit(solution)/shard_map/ppermute | solution.py:179
  89.0 8.4 %collective-permute-start.15 = (bf16[64,3072]{1,0:T(8,128)(2,1)S(1)}, bf16[64,3072]{1,0:T(8,128)(2,1)S(1)}, u32[]{:S(2)}, u32[]{:S(2)}) collective-permute-start(bf16[64,3072]{1,0:T(8,128)(2,1)S(1)} %get-tuple-element.38), channel_id=1, source_target_pairs={{0,8},{8,16},{16,24},{24,0},{1,9},{9,17},{17,25},{25,1},{2,10},{10... | collective-permute-start | bytes 1179656 | tf_op jit(solution)/shard_map/ppermute | solution.py:179
  89.2 11.9 %collective-permute-start.11 = (bf16[64,3072]{1,0:T(8,128)(2,1)}, bf16[64,3072]{1,0:T(8,128)(2,1)S(1)}, u32[]{:S(2)}, u32[]{:S(2)}) collective-permute-start(bf16[64,3072]{1,0:T(8,128)(2,1)} %get-tuple-element.32), channel_id=1, source_target_pairs={{0,8},{8,16},{16,24},{24,0},{1,9},{9,17},{17,25},{25,1},{2,10},{10... | collective-permute-start | bytes 1179656 | tf_op jit(solution)/shard_map/ppermute | solution.py:179
  89.2 11.8 %collective-permute-start.14 = (bf16[64,3072]{1,0:T(8,128)(2,1)}, bf16[64,3072]{1,0:T(8,128)(2,1)S(1)}, u32[]{:S(2)}, u32[]{:S(2)}) collective-permute-start(bf16[64,3072]{1,0:T(8,128)(2,1)} %get-tuple-element.36), channel_id=1, source_target_pairs={{0,24},{8,0},{16,8},{24,16},{1,25},{9,1},{17,9},{25,17},{2,26},{10... | collective-permute-start | bytes 1179656 | tf_op jit(solution)/shard_map/ppermute | solution.py:179
  94.6 12.2 %collective-permute-start.13 = (bf16[64,3072]{1,0:T(8,128)(2,1)S(1)}, bf16[64,3072]{1,0:T(8,128)(2,1)S(1)}, u32[]{:S(2)}, u32[]{:S(2)}) collective-permute-start(bf16[64,3072]{1,0:T(8,128)(2,1)S(1)} %relay.2), channel_id=1, source_target_pairs={{0,24},{8,0},{16,8},{24,16},{1,25},{9,1},{17,9},{25,17},{2,26},{10... | collective-permute-start | bytes 1179656 | tf_op jit(solution)/shard_map/ppermute | solution.py:179
  97.5 12.2 %collective-permute-start.16 = (bf16[64,3072]{1,0:T(8,128)(2,1)S(1)}, bf16[64,3072]{1,0:T(8,128)(2,1)}, u32[]{:S(2)}, u32[]{:S(2)}) collective-permute-start(bf16[64,3072]{1,0:T(8,128)(2,1)S(1)} %relay.3), channel_id=1, source_target_pairs={{0,8},{8,16},{16,24},{24,0},{1,9},{9,17},{17,25},{25,1},{2,10},{10... | collective-permute-start | bytes 1179656 | tf_op jit(solution)/shard_map/ppermute | solution.py:179
  112.9 19.1 %all-to-all-start.2 = ((bf16[8,8,6144]{2,1,0:T(8,128)(2,1)}), bf16[8,8,6144]{2,1,0:T(8,128)(2,1)S(1)}, u32[]{:S(2)}, u32[]{:S(2)}) async-start(bf16[8,8,6144]{2,1,0:T(8,128)(2,1)} %add_parts.1.refs_4_.refs_3_), calls=%async_computation.2 | async-start | bytes 1572864 | tf_op jit(solution)/shard_map/all_to_all | solution.py:367
  133.1 5.1 %collective-permute-start.17 = (bf16[8,6144]{1,0:T(8,128)(2,1)S(1)}, bf16[8,6144]{1,0:T(8,128)(2,1)S(1)}, u32[]{:S(2)}, u32[]{:S(2)}) collective-permute-start(bf16[8,6144]{1,0:T(8,128)(2,1)S(1)} %add_all.1.refs_0_), channel_id=1, source_target_pairs={{0,2},{1,3},{2,4},{3,5},{4,6},{5,7},{6,0},{7,1},{8,10},{9,11},{10,... | collective-permute-start | bytes 294920 | tf_op jit(solution)/shard_map/ppermute | solution.py:380
  133.9 6.8 %collective-permute-start.18 = (bf16[8,6144]{1,0:T(8,128)(2,1)S(1)}, bf16[8,6144]{1,0:T(8,128)(2,1)S(1)}, u32[]{:S(2)}, u32[]{:S(2)}) collective-permute-start(bf16[8,6144]{1,0:T(8,128)(2,1)S(1)} %add_all.1.refs_0_), channel_id=1, source_target_pairs={{0,4},{1,5},{2,6},{3,7},{4,0},{5,1},{6,2},{7,3},{8,12},{9,13},{10,... | collective-permute-start | bytes 294920 | tf_op jit(solution)/shard_map/ppermute | solution.py:380
  141.2 12.9 %collective-permute-start.20 = (bf16[32,6144]{1,0:T(8,128)(2,1)S(1)}, bf16[32,6144]{1,0:T(8,128)(2,1)S(1)}, u32[]{:S(2)}, u32[]{:S(2)}) collective-permute-start(bf16[32,6144]{1,0:T(8,128)(2,1)S(1)} %stack.3.refs_3_), channel_id=1, source_target_pairs={{0,1},{1,0},{2,3},{3,2},{4,5},{5,4},{6,7},{7,6},{8,9},{9,8},{10,11... | collective-permute-start | bytes 1179656 | tf_op jit(solution)/shard_map/ppermute | solution.py:388
  (24 other events, 216.7 us)
Sparse Core Ops, SparseCore 0:
  10.8 86.3 all-gather.1

commit v4 on v3

--- a/solution.py
+++ b/solution.py
@@ -414,7 +414,6 @@
     down_proj,
 ):
     picked = pick_part(moe_input, expert_ids)
-    picked, soft_keys, soft_values = lax.optimization_barrier((picked, soft_keys, soft_values))
     pairs = lax.all_gather(
         jnp.concatenate([soft_keys, soft_values], axis=1), CTX, axis=0, tiled=True
     )

time: 163 us -> 162 us (level)
  no operation moved by 1% of the time
where the time goes in v4:
time: 162 us; the launch traced here: 161 us
  starting transfers between devices  59 us (36%)
  waiting for transfers between devices  47.6 us (29%)
  Pallas kernels  21.1 us (13%)
  local copies, waits for them, and re-layouts  17.5 us (11%)
  between operations  14.2 us (9%)
    ppermute x17, starting transfers between devices, shift(): return lax.ppermute(a, axis, [(i, (i + by) % size) for i in range(size)])  26.7 us
    ppermute x17, waiting for transfers between devices, shift(): return lax.ppermute(a, axis, [(i, (i + by) % size) for i in range(size)])  26.6 us
    pallas_call x14, Pallas kernels, called(): pl.pallas_call(body, out_shape=out_shape, in_specs=list(specs) + [ANY] *...  20.8 us
    unnamed x48, local copies, waits for them, and re-layouts  17.5 us
    ppermute x1, starting transfers between devices, expert_part(): other = lax.ppermute(mine, 'ep', [(i, i ^ 1) for i in range(experts)])  11.4 us
    all_to_all x1, starting transfers between devices, expert_part(): got = lax.all_to_all(send, CTX, 0, 0)  6.47 us
    all_to_all x1, waiting for transfers between devices, expert_part(): sums = lax.all_to_all(sums, 'z', 0, 0)  6.3 us
    all_to_all x1, waiting for transfers between devices, expert_part(): got = lax.all_to_all(send, CTX, 0, 0)  5.93 us
  transfers between devices with their start and end apart: 25, of which 14 were waited for; matrix products, arithmetic and copies ran while one was open for 0% of the time, Pallas kernels for 12%

profile of v4, /device:TPU:1, one launch (start us, length us, event | category | flops | bytes accessed | tf_op | source)
XLA Modules:
  0.0 161.0 jit_solution(3563410001550776453)
XLA Ops:
  12.8 2.5 %collective-permute-start.1 = (bf16[8,6144]{1,0:T(8,128)(2,1)S(1)}, bf16[8,6144]{1,0:T(8,128)(2,1)S(1)}, u32[]{:S(2)}, u32[]{:S(2)}) collective-permute-start(bf16[8,6144]{1,0:T(8,128)(2,1)S(1)} %pick_tokens.1.refs_0_), channel_id=1, source_target_pairs={{0,16},{8,24},{16,0},{24,8},{1,17},{9,25},{17,1},{25,9},{2,18},{10... | collective-permute-start | bytes 294920 | tf_op jit(solution)/shard_map/ppermute | solution.py:179
  23.8 4.0 %collective-permute-start.4 = (bf16[32,6144]{1,0:T(8,128)(2,1)S(1)}, bf16[32,6144]{1,0:T(8,128)(2,1)S(1)}, u32[]{:S(2)}, u32[]{:S(2)}) collective-permute-start(bf16[32,6144]{1,0:T(8,128)(2,1)S(1)} %stack.2.refs_0_), channel_id=1, source_target_pairs={{0,224},{32,0},{64,32},{96,64},{128,96},{160,128},{192,160},{224,1... | collective-permute-start | bytes 1179656 | tf_op jit(solution)/shard_map/ppermute | solution.py:179
  27.8 8.8 %collective-permute-done.3.refs_1_ = bf16[32,6144]{1,0:T(8,128)(2,1)S(1)} collective-permute-done((bf16[32,6144]{1,0:T(8,128)(2,1)S(1)}, bf16[32,6144]{1,0:T(8,128)(2,1)S(1)}, u32[]{:S(2)}, u32[]{:S(2)}) %collective-permute-start.3) | collective-permute-done | bytes 393248 | tf_op jit(solution)/shard_map/ppermute | solution.py:179
  36.6 2.9 %collective-permute-start.6 = (bf16[32,6144]{1,0:T(8,128)(2,1)S(1)}, bf16[32,6144]{1,0:T(8,128)(2,1)}, u32[]{:S(2)}, u32[]{:S(2)}) collective-permute-start(bf16[32,6144]{1,0:T(8,128)(2,1)S(1)} %collective-permute-done.4.refs_2_), channel_id=1, source_target_pairs={{0,224},{32,0},{64,32},{96,64},{128,96},{160,128},{192,160},{224,1... | collective-permute-start | bytes 1179656 | tf_op jit(solution)/shard_map/ppermute | solution.py:179
  39.5 6.5 %all-to-all-start = ((bf16[32,32,128]{2,1,0:T(8,128)(2,1)}), bf16[32,32,128]{2,1,0:T(8,128)(2,1)S(1)}, u32[]{:S(2)}, u32[]{:S(2)}) async-start(bf16[32,32,128]{2,1,0:T(8,128)(2,1)} %get-tuple-element.21.refs_4_), calls=%async_computation | async-start | bytes 524288 | tf_op jit(solution)/shard_map/all_to_all | solution.py:323
  47.9 2.9 %collective-permute-start.8 = (bf16[32,6144]{1,0:T(8,128)(2,1)}, bf16[32,6144]{1,0:T(8,128)(2,1)S(1)}, u32[]{:S(2)}, u32[]{:S(2)}) collective-permute-start(bf16[32,6144]{1,0:T(8,128)(2,1)} %collective-permute-done.6.refs_4_), channel_id=1, source_target_pairs={{0,224},{32,0},{64,32},{96,64},{128,96},{160,128},{192,160},{224,1... | collective-permute-start | bytes 1179656 | tf_op jit(solution)/shard_map/ppermute | solution.py:179
  50.8 5.9 %all-to-all-done.refs_0_ = bf16[32,32,128]{2,1,0:T(8,128)(2,1)S(1)} async-done(((bf16[32,32,128]{2,1,0:T(8,128)(2,1)}), bf16[32,32,128]{2,1,0:T(8,128)(2,1)S(1)}, u32[]{:S(2)}, u32[]{:S(2)}) %all-to-all-start) | async-done | bytes 262176 | tf_op jit(solution)/shard_map/all_to_all | solution.py:323
  57.4 5.5 %all-to-all-start.1 = ((bf16[32,16,128]{2,1,0:T(8,128)(2,1)}), bf16[32,16,128]{2,1,0:T(8,128)(2,1)S(1)}, u32[]{:S(2)}, u32[]{:S(2)}) async-start(bf16[32,16,128]{2,1,0:T(8,128)(2,1)} %lightning_chain.1), calls=%async_computation.1 | async-start | bytes 262144 | tf_op jit(solution)/shard_map/all_to_all | solution.py:326
  65.0 2.5 %collective-permute-start.10 = (bf16[16,6144]{1,0:T(8,128)(2,1)}, bf16[16,6144]{1,0:T(8,128)(2,1)S(1)}, u32[]{:S(2)}, u32[]{:S(2)}) collective-permute-start(bf16[16,6144]{1,0:T(8,128)(2,1)} %get-tuple-element.23), channel_id=1, source_target_pairs={{0,224},{32,0},{64,32},{96,64},{128,96},{160,128},{192,160},{224,1... | collective-permute-start | bytes 589832 | tf_op jit(solution)/shard_map/ppermute | solution.py:179
  67.5 4.8 %all-to-all-done.1.refs_5_.refs_12_.refs_3_ = bf16[32,16,128]{2,1,0:T(8,128)(2,1)S(1)} async-done(((bf16[32,16,128]{2,1,0:T(8,128)(2,1)}), bf16[32,16,128]{2,1,0:T(8,128)(2,1)S(1)}, u32[]{:S(2)}, u32[]{:S(2)}) %all-to-all-start.1) | async-done | bytes 131104 | tf_op jit(solution)/shard_map/all_to_all | solution.py:326
  80.7 6.8 %feed_forward.1 = (bf16[64,3072]{1,0:T(8,128)(2,1)S(1)}, bf16[64,3072]{1,0:T(8,128)(2,1)S(1)}, bf16[64,3072]{1,0:T(8,128)(2,1)}, bf16[64,3072]{1,0:T(8,128)(2,1)...) custom-call(bf16[32,6144]{1,0:T(8,128)(2,1)S(1)} %stack.2.refs_0_, ...), custom_call_target="tpu_custom_call" | custom-call | flops 2717908992 | bytes 16908288 | tf_op jit(solution)/shard_map/feed_forward/pallas_call | solution.py:36
  89.1 2.6 %collective-permute-start.14 = (bf16[64,3072]{1,0:T(8,128)(2,1)}, bf16[64,3072]{1,0:T(8,128)(2,1)S(1)}, u32[]{:S(2)}, u32[]{:S(2)}) collective-permute-start(bf16[64,3072]{1,0:T(8,128)(2,1)} %get-tuple-element.32), channel_id=1, source_target_pairs={{0,24},{8,0},{16,8},{24,16},{1,25},{9,1},{17,9},{25,17},{2,26},{10... | collective-permute-start | bytes 1179656 | tf_op jit(solution)/shard_map/ppermute | solution.py:179
  91.7 2.9 %collective-permute-done.12.refs_1_ = bf16[64,3072]{1,0:T(8,128)(2,1)S(1)} collective-permute-done((bf16[64,3072]{1,0:T(8,128)(2,1)S(1)}, bf16[64,3072]{1,0:T(8,128)(2,1)S(1)}, u32[]{:S(2)}, u32[]{:S(2)}) %collective-permute-start.12) | collective-permute-done | bytes 393248 | tf_op jit(solution)/shard_map/ppermute | solution.py:179
  94.7 2.6 %collective-permute-start.13 = (bf16[64,3072]{1,0:T(8,128)(2,1)S(1)}, bf16[64,3072]{1,0:T(8,128)(2,1)S(1)}, u32[]{:S(2)}, u32[]{:S(2)}) collective-permute-start(bf16[64,3072]{1,0:T(8,128)(2,1)S(1)} %relay.2), channel_id=1, source_target_pairs={{0,24},{8,0},{16,8},{24,16},{1,25},{9,1},{17,9},{25,17},{2,26},{10... | collective-permute-start | bytes 1179656 | tf_op jit(solution)/shard_map/ppermute | solution.py:179
  97.5 3.4 %collective-permute-done.11.refs_2_ = bf16[64,3072]{1,0:T(8,128)(2,1)S(1)} collective-permute-done((bf16[64,3072]{1,0:T(8,128)(2,1)}, bf16[64,3072]{1,0:T(8,128)(2,1)S(1)}, u32[]{:S(2)}, u32[]{:S(2)}) %collective-permute-start.11) | collective-permute-done | bytes 393248 | tf_op jit(solution)/shard_map/ppermute | solution.py:179
  100.9 5.4 %collective-permute-done.13.refs_3_ = bf16[64,3072]{1,0:T(8,128)(2,1)S(1)} collective-permute-done((bf16[64,3072]{1,0:T(8,128)(2,1)S(1)}, bf16[64,3072]{1,0:T(8,128)(2,1)S(1)}, u32[]{:S(2)}, u32[]{:S(2)}) %collective-permute-start.13) | collective-permute-done | bytes 393248 | tf_op jit(solution)/shard_map/ppermute | solution.py:179
  106.3 3.1 %collective-permute-done.16.refs_6_ = bf16[64,3072]{1,0:T(8,128)(2,1)} collective-permute-done((bf16[64,3072]{1,0:T(8,128)(2,1)S(1)}, bf16[64,3072]{1,0:T(8,128)(2,1)}, u32[]{:S(2)}, u32[]{:S(2)}) %collective-permute-start.16) | collective-permute-done | bytes 393248 | tf_op jit(solution)/shard_map/ppermute | solution.py:179
  110.4 2.2 %add_parts.1.refs_4_.refs_3_ = bf16[8,8,6144]{2,1,0:T(8,128)(2,1)} custom-call(s32[1]{0:T(128)} %bitcast.3.refs_0_, bf16[64,3072]{1,0:T(8,128)(2,1)S(1)} %get-tuple-element.27.refs_1_, bf16[64,3072]{1,0:T(8,128)(2,1)S(1)} %collective-permute-done.11.refs_2_, bf16[64,3072]{1,0:T(8,128)(2,1)S(1)} %collective-permute-done.13.refs_3_, ...), custom_call_target="tpu_custom_call" | custom-call | tf_op jit(solution)/shard_map/add_parts/pallas_call | solution.py:36
  112.6 4.0 %all-to-all-start.2 = ((bf16[8,8,6144]{2,1,0:T(8,128)(2,1)}), bf16[8,8,6144]{2,1,0:T(8,128)(2,1)S(1)}, u32[]{:S(2)}, u32[]{:S(2)}) async-start(bf16[8,8,6144]{2,1,0:T(8,128)(2,1)} %add_parts.1.refs_4_.refs_3_), calls=%async_computation.2 | async-start | bytes 1572864 | tf_op jit(solution)/shard_map/all_to_all | solution.py:367
  118.7 2.2 %copy-done = bf16[8192,256]{1,0:T(8,128)(2,1)S(1)} copy-done((bf16[8192,256]{1,0:T(8,128)(2,1)S(1)}, bf16[8192,256]{1,0:T(8,128)(2,1)}, u32[]{:S(2)}) %copy-start) | copy-done | bytes 4194328
  120.9 4.3 %sparse_attention.1.refs_1_ = bf16[256,512]{1,0:T(8,128)(2,1)} custom-call(s32[2,8]{1,0:T(2,128)S(1)} %copy-done.21, bf16[256,512]{1,0:T(8,128)(2,1)S(1)} %copy-done.14, bf16[8192,256]{1,0:T(8,128)(2,1)S(1)} %copy-done, bf16[8,8,6144]{2,1,0:T(8,128)(2,1)} %add_parts.1.refs_4_.refs_3_), custom_call_target="tpu_custom_call" | custom-call | tf_op jit(solution)/shard_map/sparse_attention/pallas_call | solution.py:36
  125.2 6.3 %all-to-all-done.2.refs_0_ = bf16[8,8,6144]{2,1,0:T(8,128)(2,1)S(1)} async-done(((bf16[8,8,6144]{2,1,0:T(8,128)(2,1)}), bf16[8,8,6144]{2,1,0:T(8,128)(2,1)S(1)}, u32[]{:S(2)}, u32[]{:S(2)}) %all-to-all-start.2) | async-done | bytes 786464 | tf_op jit(solution)/shard_map/all_to_all | solution.py:367
  133.5 3.0 %collective-permute-start.18 = (bf16[8,6144]{1,0:T(8,128)(2,1)S(1)}, bf16[8,6144]{1,0:T(8,128)(2,1)S(1)}, u32[]{:S(2)}, u32[]{:S(2)}) collective-permute-start(bf16[8,6144]{1,0:T(8,128)(2,1)S(1)} %add_all.1.refs_0_), channel_id=1, source_target_pairs={{0,4},{1,5},{2,6},{3,7},{4,0},{5,1},{6,2},{7,3},{8,12},{9,13},{10,... | collective-permute-start | bytes 294920 | tf_op jit(solution)/shard_map/ppermute | solution.py:380
  140.3 11.4 %collective-permute-start.20 = (bf16[32,6144]{1,0:T(8,128)(2,1)S(1)}, bf16[32,6144]{1,0:T(8,128)(2,1)S(1)}, u32[]{:S(2)}, u32[]{:S(2)}) collective-permute-start(bf16[32,6144]{1,0:T(8,128)(2,1)S(1)} %stack.3.refs_3_), channel_id=1, source_target_pairs={{0,1},{1,0},{2,3},{3,2},{4,5},{5,4},{6,7},{7,6},{8,9},{9,8},{10,11... | collective-permute-start | bytes 1179656 | tf_op jit(solution)/shard_map/ppermute | solution.py:388
  (91 shorter events, 40.2 us)
Async XLA Ops:
  7.2 111.5 %all-gather.2.cloned.1.call-start = ((), (), s32[]{:S(2)}) async-start(), calls=%async_computation.3 | async-start | bytes 4325376 | tf_op jit(solution)/shard_map/all_gather | solution.py:417
  10.7 11.3 %collective-permute-start = (bf16[8,6144]{1,0:T(8,128)(2,1)S(1)}, bf16[8,6144]{1,0:T(8,128)(2,1)S(1)}, u32[]{:S(2)}, u32[]{:S(2)}) collective-permute-start(bf16[8,6144]{1,0:T(8,128)(2,1)S(1)} %pick_tokens.1.refs_0_), channel_id=1, source_target_pairs={{0,8},{8,16},{16,24},{24,0},{1,9},{9,17},{17,25},{25,1},{2,10},{10... | collective-permute-start | bytes 294920 | tf_op jit(solution)/shard_map/ppermute | solution.py:179
  12.8 9.2 %collective-permute-start.1 = (bf16[8,6144]{1,0:T(8,128)(2,1)S(1)}, bf16[8,6144]{1,0:T(8,128)(2,1)S(1)}, u32[]{:S(2)}, u32[]{:S(2)}) collective-permute-start(bf16[8,6144]{1,0:T(8,128)(2,1)S(1)} %pick_tokens.1.refs_0_), channel_id=1, source_target_pairs={{0,16},{8,24},{16,0},{24,8},{1,17},{9,25},{17,1},{25,9},{2,18},{10... | collective-permute-start | bytes 294920 | tf_op jit(solution)/shard_map/ppermute | solution.py:179
  15.3 6.7 %collective-permute-start.2 = (bf16[8,6144]{1,0:T(8,128)(2,1)S(1)}, bf16[8,6144]{1,0:T(8,128)(2,1)S(1)}, u32[]{:S(2)}, u32[]{:S(2)}) collective-permute-start(bf16[8,6144]{1,0:T(8,128)(2,1)S(1)} %pick_tokens.1.refs_0_), channel_id=1, source_target_pairs={{0,24},{8,0},{16,8},{24,16},{1,25},{9,1},{17,9},{25,17},{2,26},{10... | collective-permute-start | bytes 294920 | tf_op jit(solution)/shard_map/ppermute | solution.py:179
  22.0 14.6 %collective-permute-start.3 = (bf16[32,6144]{1,0:T(8,128)(2,1)S(1)}, bf16[32,6144]{1,0:T(8,128)(2,1)S(1)}, u32[]{:S(2)}, u32[]{:S(2)}) collective-permute-start(bf16[32,6144]{1,0:T(8,128)(2,1)S(1)} %stack.2.refs_0_), channel_id=1, source_target_pairs={{0,32},{32,64},{64,96},{96,128},{128,160},{160,192},{192,224},{224... | collective-permute-start | bytes 1179656 | tf_op jit(solution)/shard_map/ppermute | solution.py:179
  23.8 12.9 %collective-permute-start.4 = (bf16[32,6144]{1,0:T(8,128)(2,1)S(1)}, bf16[32,6144]{1,0:T(8,128)(2,1)S(1)}, u32[]{:S(2)}, u32[]{:S(2)}) collective-permute-start(bf16[32,6144]{1,0:T(8,128)(2,1)S(1)} %stack.2.refs_0_), channel_id=1, source_target_pairs={{0,224},{32,0},{64,32},{96,64},{128,96},{160,128},{192,160},{224,1... | collective-permute-start | bytes 1179656 | tf_op jit(solution)/shard_map/ppermute | solution.py:179
  36.6 11.3 %collective-permute-start.5 = (bf16[32,6144]{1,0:T(8,128)(2,1)S(1)}, bf16[32,6144]{1,0:T(8,128)(2,1)S(1)}, u32[]{:S(2)}, u32[]{:S(2)}) collective-permute-start(bf16[32,6144]{1,0:T(8,128)(2,1)S(1)} %collective-permute-done.3.refs_1_), channel_id=1, source_target_pairs={{0,32},{32,64},{64,96},{96,128},{128,160},{160,192},{192,224},{224... | collective-permute-start | bytes 1179656 | tf_op jit(solution)/shard_map/ppermute | solution.py:179
  36.6 11.3 %collective-permute-start.6 = (bf16[32,6144]{1,0:T(8,128)(2,1)S(1)}, bf16[32,6144]{1,0:T(8,128)(2,1)}, u32[]{:S(2)}, u32[]{:S(2)}) collective-permute-start(bf16[32,6144]{1,0:T(8,128)(2,1)S(1)} %collective-permute-done.4.refs_2_), channel_id=1, source_target_pairs={{0,224},{32,0},{64,32},{96,64},{128,96},{160,128},{192,160},{224,1... | collective-permute-start | bytes 1179656 | tf_op jit(solution)/shard_map/ppermute | solution.py:179
  39.5 17.2 %all-to-all-start = ((bf16[32,32,128]{2,1,0:T(8,128)(2,1)}), bf16[32,32,128]{2,1,0:T(8,128)(2,1)S(1)}, u32[]{:S(2)}, u32[]{:S(2)}) async-start(bf16[32,32,128]{2,1,0:T(8,128)(2,1)} %get-tuple-element.21.refs_4_), calls=%async_computation | async-start | bytes 524288 | tf_op jit(solution)/shard_map/all_to_all | solution.py:323
  47.9 16.2 %collective-permute-start.7 = (bf16[32,6144]{1,0:T(8,128)(2,1)S(1)}, bf16[32,6144]{1,0:T(8,128)(2,1)S(1)}, u32[]{:S(2)}, u32[]{:S(2)}) collective-permute-start(bf16[32,6144]{1,0:T(8,128)(2,1)S(1)} %collective-permute-done.5.refs_3_), channel_id=1, source_target_pairs={{0,32},{32,64},{64,96},{96,128},{128,160},{160,192},{192,224},{224... | collective-permute-start | bytes 1179656 | tf_op jit(solution)/shard_map/ppermute | solution.py:179
  47.9 16.1 %collective-permute-start.8 = (bf16[32,6144]{1,0:T(8,128)(2,1)}, bf16[32,6144]{1,0:T(8,128)(2,1)S(1)}, u32[]{:S(2)}, u32[]{:S(2)}) collective-permute-start(bf16[32,6144]{1,0:T(8,128)(2,1)} %collective-permute-done.6.refs_4_), channel_id=1, source_target_pairs={{0,224},{32,0},{64,32},{96,64},{128,96},{160,128},{192,160},{224,1... | collective-permute-start | bytes 1179656 | tf_op jit(solution)/shard_map/ppermute | solution.py:179
  57.4 14.9 %all-to-all-start.1 = ((bf16[32,16,128]{2,1,0:T(8,128)(2,1)}), bf16[32,16,128]{2,1,0:T(8,128)(2,1)S(1)}, u32[]{:S(2)}, u32[]{:S(2)}) async-start(bf16[32,16,128]{2,1,0:T(8,128)(2,1)} %lightning_chain.1), calls=%async_computation.1 | async-start | bytes 262144 | tf_op jit(solution)/shard_map/all_to_all | solution.py:326
  64.8 14.9 %collective-permute-start.9 = (bf16[16,6144]{1,0:T(8,128)(2,1)}, bf16[16,6144]{1,0:T(8,128)(2,1)S(1)}, u32[]{:S(2)}, u32[]{:S(2)}) collective-permute-start(bf16[16,6144]{1,0:T(8,128)(2,1)} %get-tuple-element.22), channel_id=1, source_target_pairs={{0,32},{32,64},{64,96},{96,128},{128,160},{160,192},{192,224},{224... | collective-permute-start | bytes 589832 | tf_op jit(solution)/shard_map/ppermute | solution.py:179
  65.0 14.7 %collective-permute-start.10 = (bf16[16,6144]{1,0:T(8,128)(2,1)}, bf16[16,6144]{1,0:T(8,128)(2,1)S(1)}, u32[]{:S(2)}, u32[]{:S(2)}) collective-permute-start(bf16[16,6144]{1,0:T(8,128)(2,1)} %get-tuple-element.23), channel_id=1, source_target_pairs={{0,224},{32,0},{64,32},{96,64},{128,96},{160,128},{192,160},{224,1... | collective-permute-start | bytes 589832 | tf_op jit(solution)/shard_map/ppermute | solution.py:179
  87.6 7.0 %collective-permute-start.12 = (bf16[64,3072]{1,0:T(8,128)(2,1)S(1)}, bf16[64,3072]{1,0:T(8,128)(2,1)S(1)}, u32[]{:S(2)}, u32[]{:S(2)}) collective-permute-start(bf16[64,3072]{1,0:T(8,128)(2,1)S(1)} %get-tuple-element.30), channel_id=1, source_target_pairs={{0,24},{8,0},{16,8},{24,16},{1,25},{9,1},{17,9},{25,17},{2,26},{10... | collective-permute-start | bytes 1179656 | tf_op jit(solution)/shard_map/ppermute | solution.py:179
  88.9 8.4 %collective-permute-start.15 = (bf16[64,3072]{1,0:T(8,128)(2,1)S(1)}, bf16[64,3072]{1,0:T(8,128)(2,1)S(1)}, u32[]{:S(2)}, u32[]{:S(2)}) collective-permute-start(bf16[64,3072]{1,0:T(8,128)(2,1)S(1)} %get-tuple-element.34), channel_id=1, source_target_pairs={{0,8},{8,16},{16,24},{24,0},{1,9},{9,17},{17,25},{25,1},{2,10},{10... | collective-permute-start | bytes 1179656 | tf_op jit(solution)/shard_map/ppermute | solution.py:179
  89.0 11.9 %collective-permute-start.11 = (bf16[64,3072]{1,0:T(8,128)(2,1)}, bf16[64,3072]{1,0:T(8,128)(2,1)S(1)}, u32[]{:S(2)}, u32[]{:S(2)}) collective-permute-start(bf16[64,3072]{1,0:T(8,128)(2,1)} %get-tuple-element.28), channel_id=1, source_target_pairs={{0,8},{8,16},{16,24},{24,0},{1,9},{9,17},{17,25},{25,1},{2,10},{10... | collective-permute-start | bytes 1179656 | tf_op jit(solution)/shard_map/ppermute | solution.py:179
  89.1 11.8 %collective-permute-start.14 = (bf16[64,3072]{1,0:T(8,128)(2,1)}, bf16[64,3072]{1,0:T(8,128)(2,1)S(1)}, u32[]{:S(2)}, u32[]{:S(2)}) collective-permute-start(bf16[64,3072]{1,0:T(8,128)(2,1)} %get-tuple-element.32), channel_id=1, source_target_pairs={{0,24},{8,0},{16,8},{24,16},{1,25},{9,1},{17,9},{25,17},{2,26},{10... | collective-permute-start | bytes 1179656 | tf_op jit(solution)/shard_map/ppermute | solution.py:179
  94.7 11.6 %collective-permute-start.13 = (bf16[64,3072]{1,0:T(8,128)(2,1)S(1)}, bf16[64,3072]{1,0:T(8,128)(2,1)S(1)}, u32[]{:S(2)}, u32[]{:S(2)}) collective-permute-start(bf16[64,3072]{1,0:T(8,128)(2,1)S(1)} %relay.2), channel_id=1, source_target_pairs={{0,24},{8,0},{16,8},{24,16},{1,25},{9,1},{17,9},{25,17},{2,26},{10... | collective-permute-start | bytes 1179656 | tf_op jit(solution)/shard_map/ppermute | solution.py:179
  97.4 12.0 %collective-permute-start.16 = (bf16[64,3072]{1,0:T(8,128)(2,1)S(1)}, bf16[64,3072]{1,0:T(8,128)(2,1)}, u32[]{:S(2)}, u32[]{:S(2)}) collective-permute-start(bf16[64,3072]{1,0:T(8,128)(2,1)S(1)} %relay.3), channel_id=1, source_target_pairs={{0,8},{8,16},{16,24},{24,0},{1,9},{9,17},{17,25},{25,1},{2,10},{10... | collective-permute-start | bytes 1179656 | tf_op jit(solution)/shard_map/ppermute | solution.py:179
  112.6 19.0 %all-to-all-start.2 = ((bf16[8,8,6144]{2,1,0:T(8,128)(2,1)}), bf16[8,8,6144]{2,1,0:T(8,128)(2,1)S(1)}, u32[]{:S(2)}, u32[]{:S(2)}) async-start(bf16[8,8,6144]{2,1,0:T(8,128)(2,1)} %add_parts.1.refs_4_.refs_3_), calls=%async_computation.2 | async-start | bytes 1572864 | tf_op jit(solution)/shard_map/all_to_all | solution.py:367
  132.6 5.0 %collective-permute-start.17 = (bf16[8,6144]{1,0:T(8,128)(2,1)S(1)}, bf16[8,6144]{1,0:T(8,128)(2,1)S(1)}, u32[]{:S(2)}, u32[]{:S(2)}) collective-permute-start(bf16[8,6144]{1,0:T(8,128)(2,1)S(1)} %add_all.1.refs_0_), channel_id=1, source_target_pairs={{0,2},{1,3},{2,4},{3,5},{4,6},{5,7},{6,0},{7,1},{8,10},{9,11},{10,... | collective-permute-start | bytes 294920 | tf_op jit(solution)/shard_map/ppermute | solution.py:380
  133.5 6.0 %collective-permute-start.18 = (bf16[8,6144]{1,0:T(8,128)(2,1)S(1)}, bf16[8,6144]{1,0:T(8,128)(2,1)S(1)}, u32[]{:S(2)}, u32[]{:S(2)}) collective-permute-start(bf16[8,6144]{1,0:T(8,128)(2,1)S(1)} %add_all.1.refs_0_), channel_id=1, source_target_pairs={{0,4},{1,5},{2,6},{3,7},{4,0},{5,1},{6,2},{7,3},{8,12},{9,13},{10,... | collective-permute-start | bytes 294920 | tf_op jit(solution)/shard_map/ppermute | solution.py:380
  140.3 12.8 %collective-permute-start.20 = (bf16[32,6144]{1,0:T(8,128)(2,1)S(1)}, bf16[32,6144]{1,0:T(8,128)(2,1)S(1)}, u32[]{:S(2)}, u32[]{:S(2)}) collective-permute-start(bf16[32,6144]{1,0:T(8,128)(2,1)S(1)} %stack.3.refs_3_), channel_id=1, source_target_pairs={{0,1},{1,0},{2,3},{3,2},{4,5},{5,4},{6,7},{7,6},{8,9},{9,8},{10,11... | collective-permute-start | bytes 1179656 | tf_op jit(solution)/shard_map/ppermute | solution.py:388
  (24 other events, 214.4 us)
Sparse Core Ops, SparseCore 0:
  10.6 86.4 all-gather.1
